TPU v7x, 256 devices: a whole 4x4x8 slice. The times are simulated.
256 devices in a mesh: layer: 8 (over z_hi, y), tile: 32 (over x, z_lo, core).
Axes of the slice: x: 4, y: 4, z: 8 (z_hi: 2, z_lo: 4; z = z_hi * 4 + z_lo), core: 2. Of those that a mesh axis runs over, the one named last changes fastest.
Arguments:
- tau: bfloat16 [1024, 57600], P(None, ('layer', 'tile')), may hold values from -6 to 6
- vvvv: bfloat16 [128, 128, 57600], P('tile', None, 'layer'), may hold values from -0.0234375 to 0.0234375
- scales: float32 [128], P('tile'), may hold values from 0.5 to 2
- tile_ids: int32 [128], replicated, may hold values from 0 to 127, as said below
- counts: int32 [32], replicated, may hold values from 1 to 4, as said below
- spin_c: int32 [48], replicated, may hold values from 0 to 1
- spin_d: int32 [1200], replicated, may hold values from 0 to 1
- pair_energy: float32 [1024], P(('layer', 'tile')), may hold values from -1.5 to -0.5
- ab_energy: float32 [128, 128], replicated, may hold values from 1 to 3
Outputs:
- amplitudes: float32 [1024, 16384], P(('layer', 'tile'))
Inputs may be any that keep to these rules, and one draw needn't show every extreme that they name: `tile_ids`: every ab tile appears exactly once; slot s of tile index t is entry t * 4 + s. The valid slots are the first counts[t] slots of tile index t; some index has all 4 valid.
All inputs are finite; a program needn't handle non-finite values.
Results may differ from a plain program's by a relative error of at most 0.0003.
Values may be sent and summed in bfloat16 or wider, within the bound.
A program may use at most 128 MiB of HBM per device.

v0:
```python
import jax
import jax.numpy as jnp
from jax import lax
from jax.sharding import PartitionSpec as P


def local(tau, vvvv, scales, tile_ids, counts, spin_c, spin_d, pair_energy, ab_energy):
    slots, width, klayer = vvvv.shape
    pairs, kpiece = tau.shape
    ntile = lax.axis_size("tile")
    nlayer = lax.axis_size("layer")
    panel = spin_c.shape[0]
    virtual = spin_d.shape[0]
    base = (lax.axis_index("layer") * ntile + lax.axis_index("tile")) * kpiece
    column = base + jnp.arange(kpiece, dtype=jnp.int32)
    c_index = column // virtual
    d_index = column % virtual
    spin_left = jnp.sum(
        jnp.where(
            c_index[:, None] == jnp.arange(panel, dtype=jnp.int32)[None, :], spin_c[None, :], 0
        ),
        axis=1,
    )
    spin_right = jnp.sum(
        jnp.where(
            d_index[:, None] == jnp.arange(virtual, dtype=jnp.int32)[None, :], spin_d[None, :], 0
        ),
        axis=1,
    )
    factor = jnp.where(spin_left == spin_right, 0.5, 1.0).astype(jnp.bfloat16)
    weighted = tau * factor[None, :]
    partial_value = jnp.einsum(
        "pk,stk->pst",
        lax.all_gather(weighted, "tile", axis=1, tiled=True),
        vvvv,
        preferred_element_type=jnp.float32,
    )
    partial_value = partial_value * scales[None, :, None]
    flat = partial_value.reshape(pairs, slots * width)
    own_pairs = pairs // (nlayer * ntile)
    reduced = lax.psum_scatter(flat, "layer", scatter_dimension=0, tiled=True)
    owned = lax.all_to_all(reduced, "tile", split_axis=0, concat_axis=1, tiled=True)
    all_slots = slots * ntile
    slot_index = jnp.arange(all_slots, dtype=jnp.int32)
    owner = slot_index // slots
    owner_count = jnp.sum(
        jnp.where(
            owner[:, None] == jnp.arange(ntile, dtype=jnp.int32)[None, :], counts[None, :], 0
        ),
        axis=1,
    )
    valid = slot_index % slots < owner_count
    onehot = ((tile_ids[:, None] == slot_index[None, :]) & valid[:, None]).astype(jnp.float32)
    residual = jnp.einsum(
        "pga,gj->pja",
        owned.reshape(own_pairs, all_slots, width),
        onehot,
        precision=lax.Precision.HIGHEST,
    )
    denom = ab_energy[None, :, :] - pair_energy[:, None, None]
    return (residual / denom).reshape(own_pairs, all_slots * width)


def solution(mesh):
    placed = (
        P(None, ("layer", "tile")),
        P("tile", None, "layer"),
        P("tile"),
        P(),
        P(),
        P(),
        P(),
        P(("layer", "tile")),
        P(),
    )
    return jax.shard_map(
        local, mesh=mesh, in_specs=placed, out_specs=P(("layer", "tile"), None), check_vma=False
    )
```

profile of v0, /device:TPU:1, one launch (start us, length us, event | category | flops | bytes accessed | tf_op | source)
XLA Modules:
  0.0 256.1 jit_solution(4001056201537388112)
XLA Ops:
  6.5 0.0 all-gather.3.cloned.1.call-start
  6.6 1.0 select_reduce_fusion
  7.6 0.7 select_reduce_fusion.1
  8.3 1.9 multiply_bitcast_fusion
  10.2 0.0 all-gather.3.cloned.1.call-update
  10.3 0.0 copy-start.1
  10.3 0.0 reduce-scatter.2.cloned.1.call-start
  10.3 96.1 %all-gather.3.cloned.1.call-done = bf16[32,225,1024]{2,1,0:T(8,128)(2,1)} async-done(((bf16[1,225,1024]{2,1,0:T(8,128)(2,1)}), bf16[32,225,1024]{2,1,0:T(8,128)(2,1)}) %all-gather.3.cloned.1.call-update) | async-done | bytes 14745616 | tf_op jit(solution)/shard_map/all_gather | solution.py:34
  106.5 12.0 %reshape.75 = bf16[7200,1024,1]{1,0,2:T(8,128)(2,1)} reshape(bf16[32,225,1024]{2,1,0:T(8,128)(2,1)} %all-gather.3.cloned.1.call-done) | data formatting | bytes 29491200
  118.4 0.0 copy-done.1
  118.4 13.5 %convolution_multiply_fusion = f32[1024,4,128]{0,2,1:T(8,128)S(1)} fusion(bf16[7200,1024,1]{1,0,2:T(8,128)(2,1)} %reshape.75, bf16[4,128,7200]{1,2,0:T(8,128)(2,1)} %param.10, f32[4]{0:T(128)S(1)} %copy-done.1), kind=kOutput, calls=%fused_computation | convolution fusion | flops 7550271488 | bytes 24215568 | tf_op jit(solution)/shard_map/pk,stk->pst/dot_general | solution.py:32
  132.0 1.9 copy.15
  133.9 0.0 reduce-scatter.2.cloned.1.call-update
  133.9 94.5 %reduce-scatter.2.cloned.1.call-done = f32[128,512]{1,0:T(8,128)} async-done(((f32[1024,512]{1,0:T(8,128)}), f32[128,512]{1,0:T(8,128)}) %reduce-scatter.2.cloned.1.call-update) | async-done | bytes 262160 | tf_op jit(solution)/shard_map/reduce_scatter | solution.py:41
  228.4 1.7 all_to_all.12
  230.1 6.5 %all-to-all-start = ((f32[32,4,512]{2,1,0:T(4,128)}), f32[32,4,512]{2,1,0:T(4,128)S(1)}, u32[]{:S(2)}, u32[]{:S(2)}) async-start(f32[32,4,512]{2,1,0:T(4,128)} %all_to_all.12), calls=%async_computation.1 | async-start | bytes 524288 | tf_op jit(solution)/shard_map/all_to_all | solution.py:42
  236.7 0.0 copy-done.2
  236.7 0.1 select_reduce_fusion.2
  236.8 11.2 %all-to-all-done = f32[32,4,512]{2,1,0:T(4,128)S(1)} async-done(((f32[32,4,512]{2,1,0:T(4,128)}), f32[32,4,512]{2,1,0:T(4,128)S(1)}, u32[]{:S(2)}, u32[]{:S(2)}) %all-to-all-start) | async-done | bytes 262176 | tf_op jit(solution)/shard_map/all_to_all | solution.py:42
  248.0 0.1 copy.16
  248.1 0.0 copy-done
  248.1 0.0 copy-done.3
  248.1 0.3 fusion.1
  248.4 0.9 copy.19
  (10 shorter events, 0.1 us)
Async XLA Ops:
  6.5 99.9 %all-gather.3.cloned.1.call-start = ((), (), s32[]{:S(2)}) async-start(), calls=%async_computation.3 | async-start | bytes 15679488 | tf_op jit(solution)/shard_map/all_gather | solution.py:34
  10.3 108.2 %copy-start.1 = (f32[4]{0:T(128)S(1)}, f32[4]{0:T(128)}, u32[]{:S(2)}) copy-start(f32[4]{0:T(128)} %param.11) | copy-start | bytes 52
  10.3 218.1 %reduce-scatter.2.cloned.1.call-start = ((), (), s32[]{:S(2)}) async-start(), calls=%async_computation.2 | async-start | bytes 2359296 | tf_op jit(solution)/shard_map/reduce_scatter | solution.py:41
  133.9 102.8 %copy-start.2 = (s32[32]{0:T(128)S(1)}, s32[32]{0:T(128)}, u32[]{:S(2)}) copy-start(s32[32]{0:T(128)} %param.13) | copy-start | bytes 388
  133.9 114.2 %copy-start = (f32[128,128]{1,0:T(8,128)S(1)}, f32[128,128]{1,0:T(8,128)}, u32[]{:S(2)}) copy-start(f32[128,128]{1,0:T(8,128)} %param.17) | copy-start | bytes 196612
  133.9 114.2 %copy-start.3 = (f32[4]{0:T(128)S(1)}, f32[4]{0:T(128)}, u32[]{:S(2)}) copy-start(f32[4]{0:T(128)} %param.16) | copy-start | bytes 52
  133.9 114.2 %copy-start.4 = (s32[128]{0:T(128)S(1)}, s32[128]{0:T(128)}, u32[]{:S(2)}) copy-start(s32[128]{0:T(128)} %param.12) | copy-start | bytes 1540
  230.1 17.8 %all-to-all-start = ((f32[32,4,512]{2,1,0:T(4,128)}), f32[32,4,512]{2,1,0:T(4,128)S(1)}, u32[]{:S(2)}, u32[]{:S(2)}) async-start(f32[32,4,512]{2,1,0:T(4,128)} %all_to_all.12), calls=%async_computation.1 | async-start | bytes 524288 | tf_op jit(solution)/shard_map/all_to_all | solution.py:42
Sparse Core Ops, SparseCore 0:
  10.4 96.0 all-gather.2
  134.0 94.3 reduce-scatter.1
where the time goes:
time: 256 us
  waiting for transfers between devices  202 us (79%)
  local copies, waits for them, and re-layouts  16.6 us (6%)
  matrix products  13.8 us (5%)
  between operations  13.5 us (5%)
  starting transfers between devices  6.59 us (3%)
  other arithmetic  3.78 us (1%)
    all_gather x1, waiting for transfers between devices, local(): lax.all_gather(weighted, 'tile', axis=1, tiled=True)  96.1 us
    reduce_scatter x1, waiting for transfers between devices, local(): reduced = lax.psum_scatter(flat, 'layer', scatter_dimension=0, tiled=True)  94.5 us
    dot_general x1, matrix products, local(): jnp.einsum('pk,stk->pst', lax.all_gather(weighted, 'tile', axis=1, tiled=...  13.5 us
    unnamed x12, local copies, waits for them, and re-layouts  12.9 us
    all_to_all x1, waiting for transfers between devices, local(): lax.all_to_all(reduced, 'tile', split_axis=0, concat_axis=1, tiled=True)  11.2 us
    all_to_all x1, starting transfers between devices, local(): lax.all_to_all(reduced, 'tile', split_axis=0, concat_axis=1, tiled=True)  6.55 us
  transfers between devices with their start and end apart: 3, of which 3 were waited for; matrix products, arithmetic and copies ran while one was open for 0% of the time, Pallas kernels for 0%

commit v1 on v0

v1 whole, which is shorter than its diff:
```python
import functools

import jax
import jax.numpy as jnp
from jax import lax
from jax.experimental import pallas as pl
from jax.experimental.pallas import tpu as pltpu
from jax.sharding import PartitionSpec as P

MESH = pl.DeviceIdType.MESH

NX, NZ, NK, NY, NH = 4, 4, 2, 4, 2
LANES = 128
CHUNKS = 8
ROWS = 240
PAD = 256
A_ROWS = 192


def ladder_kernel(
    tau_ref,
    v_hbm,
    scales_ref,
    spin_c_ref,
    spin_d_ref,
    out_ref,
    t_buf,
    v_buf,
    vt_buf,
    w_buf,
    acc,
    r_buf,
    y_buf,
    q_buf,
    z_buf,
    s_buf,
    v_sem,
    az_s,
    az_r,
    ax_s,
    ax_r,
    bx_s,
    bx_r,
    bz_s,
    bz_r,
    sa_s,
    sa_r,
    sb_s,
    sb_r,
    y_s,
    y_r,
    z_s,
    z_r,
    x_s,
    x_r,
):
    layer = lax.axis_index("layer")
    tile = lax.axis_index("tile")
    xx, zz, kk = tile // 8, (tile // 2) % 4, tile % 2
    hh, yy = layer // 4, layer % 4
    kpiece = tau_ref.shape[0]
    klayer = v_hbm.shape[1]
    virtual = spin_d_ref.shape[1]
    panel = spin_c_ref.shape[1]

    def xdev(x):
        return (layer, x * 8 + zz * 2 + kk)

    def zdev(z):
        return (layer, xx * 8 + z * 2 + kk)

    sib = (layer, xx * 8 + zz * 2 + (1 - kk))

    def ydev(y):
        return (hh * 4 + y, tile)

    def ring(h, z, k):
        return (h * 4 + yy, xx * 8 + z * 2 + k)

    barrier = pltpu.get_barrier_semaphore()

    def greet(dev):
        pl.semaphore_signal(barrier, inc=1, device_id=dev, device_id_type=MESH)

    for step in range(1, NX):
        greet(xdev((xx + step) % NX))
    for step in range(1, NY):
        greet(ydev((yy + step) % NY))
    greet(sib)
    for step in range(1, NH * NZ):
        place = (hh * NZ + zz + step) % (NH * NZ)
        for core in range(NK):
            greet(ring(place // NZ, place % NZ, core))

    v_copy = pltpu.make_async_copy(v_hbm, v_buf.at[:, pl.ds(0, klayer)], v_sem)
    v_copy.start()
    v_buf[:, klayer:, :] = jnp.zeros((v_buf.shape[0], v_buf.shape[1] - klayer, 128), v_buf.dtype)

    start = (kpiece * tile) // 16 * 16
    offset = kpiece * tile - start
    base = layer * klayer + start
    c_first = base // virtual
    d_first = base - c_first * virtual
    row = lax.broadcasted_iota(jnp.int32, (ROWS, 1), 0)
    d_index = row + d_first
    over = d_index >= virtual
    d_index = jnp.where(over, d_index - virtual, d_index)
    c_index = jnp.where(over, c_first + 1, c_first)
    d_iota = lax.broadcasted_iota(jnp.int32, (ROWS, virtual), 1)
    c_iota = lax.broadcasted_iota(jnp.int32, (ROWS, panel), 1)
    spin_right = jnp.sum(jnp.where(d_iota == d_index, spin_d_ref[...], 0).astype(jnp.float32), axis=1, keepdims=True)
    spin_left = jnp.sum(jnp.where(c_iota == c_index, spin_c_ref[...], 0).astype(jnp.float32), axis=1, keepdims=True)
    factor = jnp.where(spin_left == spin_right, 0.5, 1.0)
    shift = (
        lax.broadcasted_iota(jnp.int32, (ROWS, kpiece), 0) - offset
        == lax.broadcasted_iota(jnp.int32, (ROWS, kpiece), 1)
    )
    placed = jnp.dot(
        shift.astype(jnp.float32).astype(jnp.bfloat16), tau_ref[...], preferred_element_type=jnp.float32
    )
    w_buf[...] = (placed * factor).astype(jnp.bfloat16)

    def clear(step, carry):
        t_buf[step // 32, step // 8 % 4, step // 2 % 4, step % 2, ROWS:, :] = jnp.zeros((PAD - ROWS, LANES), jnp.bfloat16)
        return carry

    lax.fori_loop(0, CHUNKS * NX * NZ * NK, clear, 0)

    pl.semaphore_wait(barrier, (NX - 1) + (NY - 1) + 1 + (NH * NZ - 1) * NK)

    part_a = pl.ds(0, A_ROWS)
    part_b = pl.ds(A_ROWS, ROWS - A_ROWS)

    def copy(src, dst, ssem, rsem, dev):
        return pltpu.make_async_remote_copy(
            src_ref=src, dst_ref=dst, send_sem=ssem, recv_sem=rsem, device_id=dev, device_id_type=MESH
        )

    def same(ref, ssem, rsem, dev):
        return copy(ref, ref, ssem, rsem, dev)

    def up(c, z0):
        return same(t_buf.at[c, xx, z0, kk, part_a], az_s.at[c, z0, 0], az_r.at[c, z0], zdev(zz + 1))

    def down(c, z0):
        return same(t_buf.at[c, xx, z0, kk, part_a], az_s.at[c, z0, 1], az_r.at[c, z0], zdev(zz - 1))

    def b_up(c, z0):
        return same(t_buf.at[c, :, z0, kk, part_b], bz_s.at[c, z0, 0], bz_r.at[c, z0], zdev(zz + 1))

    def b_down(c, z0):
        return same(t_buf.at[c, :, z0, kk, part_b], bz_s.at[c, z0, 1], bz_r.at[c, z0], zdev(zz - 1))

    def turn(c, z0):
        return 1 - 2 * ((c + z0) % 2)

    def ax(c, z0, way):
        if way == 2:
            s = turn(c, z0)
            return same(
                t_buf.at[c, (xx - s + 4) % 4, z0, kk, part_a], ax_s.at[c, z0, 2], ax_r.at[c, z0, 2], xdev((xx + s + 4) % 4)
            )
        s = 1 - 2 * way
        return same(t_buf.at[c, xx, z0, kk, part_a], ax_s.at[c, z0, way], ax_r.at[c, z0, way], xdev((xx + s + 4) % 4))

    def ax_in(c, z0, way):
        source = (xx + (3, 1, 2)[way]) % 4
        return same(t_buf.at[c, source, z0, kk, part_a], ax_s.at[c, z0, way], ax_r.at[c, z0, way], xdev(source))

    def bx(c, way):
        if way == 2:
            s = turn(c, 0)
            return same(t_buf.at[c, (xx - s + 4) % 4, zz, kk, part_b], bx_s.at[c, 2], bx_r.at[c, 2], xdev((xx + s + 4) % 4))
        s = 1 - 2 * way
        return same(t_buf.at[c, xx, zz, kk, part_b], bx_s.at[c, way], bx_r.at[c, way], xdev((xx + s + 4) % 4))

    def bx_in(c, way):
        source = (xx + (3, 1, 2)[way]) % 4
        return same(t_buf.at[c, source, zz, kk, part_b], bx_s.at[c, way], bx_r.at[c, way], xdev(source))

    def sa(c, z0, core):
        return same(t_buf.at[c, :, z0, core, part_a], sa_s.at[c, z0], sa_r.at[c, z0], sib)

    def sb(c, z0, core):
        return same(t_buf.at[c, :, z0, core, part_b], sb_s.at[c, z0], sb_r.at[c, z0], sib)

    def sides(distance, act):
        for sign in (-1, 1):
            z0 = zz + sign * distance

            @pl.when((z0 >= 0) & (z0 < NZ))
            def _():
                act(z0, sign)

    def pass_on(z0, sign, send_up, send_down):
        def go(fn, edge):
            @pl.when(edge)
            def _():
                fn()

        if sign <= 0:
            go(send_up, zz < NZ - 1)
        if sign >= 0:
            go(send_down, zz > 0)

    def z_step(c, distance):
        def act(z0, sign):
            up(c, z0).wait_recv()
            pass_on(z0, sign, lambda: up(c, z0).start(), lambda: down(c, z0).start())
            ax(c, z0, 0).start()
            ax(c, z0, 1).start()

        sides(distance, act)

    def far_step(c, distance):
        def act(z0, sign):
            ax_in(c, z0, 0).wait_recv()
            ax_in(c, z0, 1).wait_recv()
            ax(c, z0, 2).start()

        act(zz, 0) if distance == 0 else sides(distance, act)

    def row_step(c, distance):
        def act(z0, sign):
            ax_in(c, z0, 2).wait_recv()
            sa(c, z0, kk).start()

        act(zz, 0) if distance == 0 else sides(distance, act)

    def b_step(c, distance):
        def act(z0, sign):
            if distance == 0:
                bx_in(c, 2).wait_recv()
            else:
                b_up(c, z0).wait_recv()
            pass_on(z0, sign, lambda: b_up(c, z0).start(), lambda: b_down(c, z0).start())
            sb(c, z0, kk).start()

        act(zz, 0) if distance == 0 else sides(distance, act)

    def own_step(c):
        q = lax.broadcasted_iota(jnp.int32, (1, LANES), 1)
        q_y, q_h, q_z, q_x = q // 32, q // 16 % 2, q // 4 % 4, q % 4
        pair = (q_h * 4 + q_y) * 128 + (q_x * 8 + q_z * 2 + c % 2) * 4 + c // 2
        pick = lax.broadcasted_iota(jnp.int32, (tau_ref.shape[1], LANES), 0) == pair
        block = jnp.dot(
            w_buf[...], pick.astype(jnp.float32).astype(jnp.bfloat16), preferred_element_type=jnp.float32
        )
        t_buf[c, xx, zz, kk, 0:ROWS, :] = block.astype(jnp.bfloat16)
        pass_on(zz, 0, lambda: up(c, zz).start(), lambda: down(c, zz).start())
        bx(c, 0).start()
        bx(c, 1).start()
        ax(c, zz, 0).start()
        ax(c, zz, 1).start()

    def bx_step(c):
        bx_in(c, 0).wait_recv()
        bx_in(c, 1).wait_recv()
        bx(c, 2).start()

    def turn_v(step):
        def one(i, carry):
            t = step * 8 + i
            first = pl.multiple_of((kpiece * t) // 16 * 16, 16)
            lanes = pl.ds(pl.multiple_of(t * PAD, PAD), PAD)
            for s in range(v_buf.shape[0]):
                vt_buf[s * 128 : (s + 1) * 128, lanes] = v_buf[s, pl.ds(first, PAD), :].T
            return carry

        lax.fori_loop(0, 8, one, 0)

    def sib_wait(c):
        def one(z0, carry):
            sa(c, z0, 1 - kk).wait_recv()
            sb(c, z0, 1 - kk).wait_recv()
            return carry

        lax.fori_loop(0, NZ, one, 0)

    def multiply(c, x):
        block = t_buf[c, x].reshape(NZ * NK * PAD, LANES)
        product = jnp.dot(
            vt_buf[:, x * NZ * NK * PAD : (x + 1) * NZ * NK * PAD], block, preferred_element_type=jnp.float32
        )
        if x == 0:
            acc[...] = product
        else:
            acc[...] += product

    def y_out(c, step):
        other = (yy + step) % NY
        rows = pl.ds(pl.multiple_of(other * 32, 32), 32)
        return copy(r_buf.at[c, rows], y_buf.at[c, 3 - step], y_s.at[c, step - 1], y_r.at[c, 3 - step], ydev(other))

    def y_in(c, slot):
        return copy(y_buf.at[c, slot], y_buf.at[c, slot], y_s.at[c, slot], y_r.at[c, slot], ydev((yy + slot + 1) % NY))

    def y_step(c):
        for s in range(v_buf.shape[0]):
            r_buf[c, :, s * 128 : (s + 1) * 128] = (acc[s * 128 : (s + 1) * 128, :] * scales_ref[s]).T
        for step in (2, 1, 3):
            y_out(c, step).start()

    def z_out(c, place):
        return copy(
            q_buf.at[c, place],
            z_buf.at[c // 2, (hh * NZ + zz) * NK + kk],
            z_s.at[c, place],
            z_r.at[c // 2, (hh * NZ + zz) * NK + kk],
            ring(place // NZ, place % NZ, c % 2),
        )

    def z_in(j, source):
        return copy(z_buf.at[j, source], z_buf.at[j, source], z_s.at[0, 0], z_r.at[j, source], sib)

    def zs_step(c):
        for slot in range(3):
            y_in(c, slot).wait_recv()
        mine = r_buf[c, pl.ds(pl.multiple_of(yy * 32, 32), 32), :]
        total = mine + y_buf[c, 0] + y_buf[c, 1] + y_buf[c, 2]
        for place in range(NH * NZ):
            q_buf[c, place] = total[place * 4 : place * 4 + 4, :]

        @pl.when(kk == c % 2)
        def _():
            z_buf[c // 2, (hh * NZ + zz) * NK + kk] = q_buf[c, hh * NZ + zz]

        @pl.when(kk != c % 2)
        def _():
            z_out(c, hh * NZ + zz).start()

        def one(step, carry):
            z_out(c, (hh * NZ + zz + step) % (NH * NZ)).start()
            return carry

        lax.fori_loop(1, NH * NZ, one, 0)

    def x_out(j, step):
        other = (xx + step) % NX
        return copy(s_buf.at[j, other], out_ref.at[j, xx], x_s.at[j, step - 1], x_r.at[j, 3 - step], xdev(other))

    def x_in(j, slot):
        source = (xx + slot + 1) % NX
        return copy(out_ref.at[j, source], out_ref.at[j, source], x_s.at[j, slot], x_r.at[j, slot], xdev(source))

    def xs_step(c):
        j = c // 2

        @pl.when(kk == c % 2)
        def _():
            def one(source, carry):
                @pl.when(source != (hh * NZ + zz) * NK + kk)
                def _():
                    z_in(j, source).wait_recv()

                return carry

            lax.fori_loop(0, NH * NZ * NK, one, 0)
            for source in range(NZ * NK):
                both = z_buf[j, source] + z_buf[j, NZ * NK + source]
                for x in range(NX):
                    s_buf[j, x, source : source + 1, :] = both[x : x + 1, :]
            for step in (2, 1, 3):
                x_out(j, step).start()
            out_ref[j, xx] = s_buf[j, xx]

    def when_in(c, act):
        @pl.when((c >= 0) & (c < CHUNKS))
        def _():
            act()

    own_step(0)

    def tick(tau, carry):
        when_in(tau + 1, lambda: own_step(tau + 1))
        when_in(tau - 8, lambda: xs_step(tau - 8))
        when_in(tau - 7, lambda: zs_step(tau - 7))
        c = tau - 6

        when_in(c, lambda: sib_wait(c))
        when_in(tau - 5, lambda: (b_step(tau - 5, 3), row_step(tau - 5, 3)))
        when_in(c, lambda: multiply(c, 0))
        when_in(tau - 4, lambda: (b_step(tau - 4, 2), row_step(tau - 4, 2), far_step(tau - 4, 3)))
        when_in(c, lambda: multiply(c, 1))
        when_in(
            tau - 3,
            lambda: (b_step(tau - 3, 1), row_step(tau - 3, 1), far_step(tau - 3, 2), z_step(tau - 3, 3)),
        )
        when_in(c, lambda: multiply(c, 2))
        when_in(
            tau - 2,
            lambda: (b_step(tau - 2, 0), row_step(tau - 2, 0), far_step(tau - 2, 1), z_step(tau - 2, 2)),
        )
        when_in(c, lambda: multiply(c, 3))
        when_in(tau - 1, lambda: (bx_step(tau - 1), z_step(tau - 1, 1), far_step(tau - 1, 0)))
        when_in(c, lambda: y_step(c))

        @pl.when(tau == 0)
        def _():
            v_copy.wait()

        @pl.when(tau < 4)
        def _():
            turn_v(tau)

        return carry

    lax.fori_loop(0, CHUNKS + 8, tick, 0)

    def last(c, carry):
        j = c // 2

        @pl.when(kk == c % 2)
        def _():
            for slot in range(3):
                x_in(j, slot).wait_recv()
            for step in range(1, NX):
                x_out(j, step).wait_send()

        @pl.when(kk != c % 2)
        def _():
            z_out(c, hh * NZ + zz).wait_send()

        def one(step, carry):
            z_out(c, (hh * NZ + zz + step) % (NH * NZ)).wait_send()
            return carry

        lax.fori_loop(1, NH * NZ, one, 0)
        for step in range(1, NY):
            y_out(c, step).wait_send()
        for way in range(3):
            bx(c, way).wait_send()

        def rows(z0, carry):
            for way in range(3):
                ax(c, z0, way).wait_send()
            sa(c, z0, kk).wait_send()
            sb(c, z0, kk).wait_send()

            @pl.when((z0 <= zz) & (zz < NZ - 1))
            def _():
                up(c, z0).wait_send()
                b_up(c, z0).wait_send()

            @pl.when((z0 >= zz) & (zz > 0))
            def _():
                down(c, z0).wait_send()
                b_down(c, z0).wait_send()

            return carry

        lax.fori_loop(0, NZ, rows, 0)
        return carry

    lax.fori_loop(0, CHUNKS, last, 0)


def local(tau, vvvv, scales, tile_ids, counts, spin_c, spin_d, pair_energy, ab_energy):
    slots, width, klayer = vvvv.shape
    pairs, kpiece = tau.shape
    ntile = lax.axis_size("tile")
    nlayer = lax.axis_size("layer")
    own_pairs = pairs // (nlayer * ntile)
    all_slots = slots * ntile
    vmem = pl.BlockSpec(memory_space=pltpu.VMEM)
    bf16, f32 = jnp.bfloat16, jnp.float32
    dma = pltpu.SemaphoreType.DMA
    owned = pl.pallas_call(
        ladder_kernel,
        out_shape=jax.ShapeDtypeStruct((own_pairs, NX, NZ * NK, slots * width), f32),
        in_specs=[vmem, pl.BlockSpec(memory_space=pl.ANY), pl.BlockSpec(memory_space=pltpu.SMEM), vmem, vmem],
        out_specs=vmem,
        scratch_shapes=[
            pltpu.VMEM((CHUNKS, NX, NZ, NK, PAD, LANES), bf16),
            pltpu.VMEM((slots, klayer + 16, width), bf16),
            pltpu.VMEM((slots * width, ntile * PAD), bf16),
            pltpu.VMEM((ROWS, pairs), bf16),
            pltpu.VMEM((slots * width, LANES), f32),
            pltpu.VMEM((CHUNKS, LANES, slots * width), f32),
            pltpu.VMEM((CHUNKS, NY - 1, LANES // NY, slots * width), f32),
            pltpu.VMEM((CHUNKS, NH * NZ, NX, slots * width), f32),
            pltpu.VMEM((own_pairs, NH * NZ * NK, NX, slots * width), f32),
            pltpu.VMEM((own_pairs, NX, NZ * NK, slots * width), f32),
            dma,
            dma((CHUNKS, NZ, 2)),
            dma((CHUNKS, NZ)),
            dma((CHUNKS, NZ, 3)),
            dma((CHUNKS, NZ, 3)),
            dma((CHUNKS, 3)),
            dma((CHUNKS, 3)),
            dma((CHUNKS, NZ, 2)),
            dma((CHUNKS, NZ)),
            dma((CHUNKS, NZ)),
            dma((CHUNKS, NZ)),
            dma((CHUNKS, NZ)),
            dma((CHUNKS, NZ)),
            dma((CHUNKS, 3)),
            dma((CHUNKS, 3)),
            dma((CHUNKS, NH * NZ)),
            dma((own_pairs, NH * NZ * NK)),
            dma((own_pairs, 3)),
            dma((own_pairs, 3)),
        ],
        compiler_params=pltpu.CompilerParams(
            collective_id=0, has_side_effects=True, vmem_limit_bytes=56 * 1024 * 1024
        ),
        name="ladder",
    )(tau.T, jnp.swapaxes(vvvv, 1, 2), scales, spin_c[None, :], spin_d[None, :])
    slot_index = jnp.arange(all_slots, dtype=jnp.int32)
    owner = slot_index // slots
    owner_count = jnp.sum(
        jnp.where(owner[:, None] == jnp.arange(ntile, dtype=jnp.int32)[None, :], counts[None, :], 0), axis=1
    )
    valid = slot_index % slots < owner_count
    onehot = ((tile_ids[:, None] == slot_index[None, :]) & valid[:, None]).astype(jnp.float32)
    residual = jnp.einsum(
        "pga,gj->pja",
        owned.reshape(own_pairs, all_slots, width),
        onehot,
        precision=lax.Precision.HIGHEST,
    )
    denom = ab_energy[None, :, :] - pair_energy[:, None, None]
    return (residual / denom).reshape(own_pairs, all_slots * width)


def solution(mesh):
    placed = (
        P(None, ("layer", "tile")),
        P("tile", None, "layer"),
        P("tile"),
        P(),
        P(),
        P(),
        P(),
        P(("layer", "tile")),
        P(),
    )
    return jax.shard_map(
        local, mesh=mesh, in_specs=placed, out_specs=P(("layer", "tile"), None), check_vma=False
    )
```

time: 256 us -> 143 us (0.56)
  waiting for transfers between devices: 202 us -> 0 us
  Pallas kernels: 0 us -> 138 us
  matrix products: 13.8 us -> 0.3 us
  local copies, waits for them, and re-layouts: 16.6 us -> 3.15 us
  between operations: 13.5 us -> 0.06 us
  starting transfers between devices: 6.59 us -> 0 us
  other arithmetic: 3.78 us -> 0.8 us
    pallas_call x0 -> x1, Pallas kernels: none -> 138 us  [local(): pl.pallas_call(ladder_kernel, out_shape=jax.ShapeDtypeStruct((own_pairs,...]
    all_gather x1 -> x0, waiting for transfers between devices: 96.1 us -> none  [local(): lax.all_gather(weighted, 'tile', axis=1, tiled=True)]
    reduce_scatter x1 -> x0, waiting for transfers between devices: 94.5 us -> none  [local(): reduced = lax.psum_scatter(flat, 'layer', scatter_dimension=0, tiled=True)]
    dot_general x1 -> x0, matrix products: 13.5 us -> none  [local(): jnp.einsum('pk,stk->pst', lax.all_gather(weighted, 'tile', axis=1, tiled=...]
    unnamed x12 -> x7, local copies, waits for them, and re-layouts: 12.9 us -> 0.88 us
    all_to_all x1 -> x0, waiting for transfers between devices: 11.2 us -> none  [local(): lax.all_to_all(reduced, 'tile', split_axis=0, concat_axis=1, tiled=True)]
    all_to_all x1 -> x0, starting transfers between devices: 6.55 us -> none  [local(): lax.all_to_all(reduced, 'tile', split_axis=0, concat_axis=1, tiled=True)]
  transfers between devices with their start and end apart: 3 -> 0, of which waited for: 3 -> 0; matrix products, arithmetic and copies ran while one was open for 0% -> 0% of each run, Pallas kernels for 0% -> 0%
where the time goes in v1:
time: 143 us
  Pallas kernels  138 us (97%)
  local copies, waits for them, and re-layouts  3.15 us (2%)
    pallas_call x1, Pallas kernels, local(): pl.pallas_call(ladder_kernel, out_shape=jax.ShapeDtypeStruct((own_pairs,...  138 us

profile of v1, /device:TPU:1, one launch (start us, length us, event | category | flops | bytes accessed | tf_op | source)
XLA Modules:
  0.0 142.7 jit_solution(6384519954413671064)
XLA Ops:
  0.0 0.0 copy-start
  0.0 0.0 copy-start.1
  0.0 0.0 copy-start.2
  0.0 0.8 select_reduce_fusion
  0.8 1.3 broadcast_in_dim.29.spin_d_ref
  2.1 138.4 %ladder.1 = f32[4,4,8,512]{3,2,1,0:T(8,128)} custom-call(bf16[225,1024]{1,0:T(8,128)(2,1)} %bitcast.21, bf16[4,7200,128]{2,1,0:T(8,128)(2,1)} %bitcast.20, f32[4]{0:T(128)} %scales_ref.1, s32[1,48]{1,0:T(1,128)} %bitcast.22, s32[1,1200]{1,0:T(1,128)} %broadcast_in_dim.29.spin_d_ref), custom_call_target="tpu_custom_call" | custom-call | tf_op jit(solution)/shard_map/ladder/pallas_call | solution.py:468
  140.5 1.0 reshape.35
  141.4 0.0 copy-done
  141.5 0.0 copy-done.1
  141.5 0.0 copy-done.2
  141.5 0.3 fusion.1
  141.8 0.9 copy.12
  (2 shorter events, 0.0 us)
Async XLA Ops:
  0.0 141.4 %copy-start = (f32[128,128]{1,0:T(8,128)S(1)}, f32[128,128]{1,0:T(8,128)}, u32[]{:S(2)}) copy-start(f32[128,128]{1,0:T(8,128)} %param.17) | copy-start | bytes 196612
  0.0 141.5 %copy-start.1 = (f32[4]{0:T(128)S(1)}, f32[4]{0:T(128)}, u32[]{:S(2)}) copy-start(f32[4]{0:T(128)} %param.16) | copy-start | bytes 52
  0.0 141.5 %copy-start.2 = (s32[128]{0:T(128)S(1)}, s32[128]{0:T(128)}, u32[]{:S(2)}) copy-start(s32[128]{0:T(128)} %param.12) | copy-start | bytes 1540

commit v2 on v1

v2 whole, which is shorter than its diff:
```python
import functools

import jax
import jax.numpy as jnp
from jax import lax
from jax.experimental import pallas as pl
from jax.experimental.pallas import tpu as pltpu
from jax.sharding import PartitionSpec as P

MESH = pl.DeviceIdType.MESH

NX, NZ, NK, NY, NH = 4, 4, 2, 4, 2
LANES = 128
CHUNKS = 8
ROWS = 240
PAD = 256
A_ROWS = 192


def ladder_kernel(
    tau_ref,
    v_hbm,
    scales_ref,
    spin_c_ref,
    spin_d_ref,
    out_ref,
    t_buf,
    v_buf,
    vt_buf,
    w_buf,
    acc,
    r_buf,
    y_buf,
    q_buf,
    z_buf,
    s_buf,
    v_sem,
    send_sem,
    az_r,
    ax_r,
    bx_r,
    bz_r,
    sib_r,
    y_r,
    z_r,
    x_r,
):
    layer = lax.axis_index("layer")
    tile = lax.axis_index("tile")
    xx, zz, kk = tile // 8, (tile // 2) % 4, tile % 2
    hh, yy = layer // 4, layer % 4
    kpiece = tau_ref.shape[0]
    klayer = v_hbm.shape[1]
    virtual = spin_d_ref.shape[1]
    panel = spin_c_ref.shape[1]

    def xdev(x):
        return (layer, x * 8 + zz * 2 + kk)

    def zdev(z):
        return (layer, xx * 8 + z * 2 + kk)

    sib = (layer, xx * 8 + zz * 2 + (1 - kk))

    def ydev(y):
        return (hh * 4 + y, tile)

    def ring(h, z, k):
        return (h * 4 + yy, xx * 8 + z * 2 + k)

    barrier = pltpu.get_barrier_semaphore()

    def greet(dev):
        pl.semaphore_signal(barrier, inc=1, device_id=dev, device_id_type=MESH)

    for step in range(1, NX):
        greet(xdev((xx + step) % NX))
    for step in range(1, NY):
        greet(ydev((yy + step) % NY))
    greet(sib)
    for step in range(1, NH * NZ):
        place = (hh * NZ + zz + step) % (NH * NZ)
        for core in range(NK):
            greet(ring(place // NZ, place % NZ, core))

    v_copy = pltpu.make_async_copy(v_hbm, v_buf.at[:, pl.ds(0, klayer)], v_sem)
    v_copy.start()
    v_buf[:, klayer:, :] = jnp.zeros((v_buf.shape[0], v_buf.shape[1] - klayer, 128), v_buf.dtype)

    start = (kpiece * tile) // 16 * 16
    offset = kpiece * tile - start
    base = layer * klayer + start
    c_first = base // virtual
    d_first = base - c_first * virtual
    row = lax.broadcasted_iota(jnp.int32, (ROWS, 1), 0)
    d_index = row + d_first
    over = d_index >= virtual
    d_index = jnp.where(over, d_index - virtual, d_index)
    c_index = jnp.where(over, c_first + 1, c_first)
    d_iota = lax.broadcasted_iota(jnp.int32, (ROWS, virtual), 1)
    c_iota = lax.broadcasted_iota(jnp.int32, (ROWS, panel), 1)
    spin_right = jnp.sum(jnp.where(d_iota == d_index, spin_d_ref[...], 0).astype(jnp.float32), axis=1, keepdims=True)
    spin_left = jnp.sum(jnp.where(c_iota == c_index, spin_c_ref[...], 0).astype(jnp.float32), axis=1, keepdims=True)
    factor = jnp.where(spin_left == spin_right, 0.5, 1.0)
    shift = (
        lax.broadcasted_iota(jnp.int32, (ROWS, kpiece), 0) - offset
        == lax.broadcasted_iota(jnp.int32, (ROWS, kpiece), 1)
    )
    placed = jnp.dot(
        shift.astype(jnp.float32).astype(jnp.bfloat16), tau_ref[...], preferred_element_type=jnp.float32
    )
    w_buf[...] = (placed * factor).astype(jnp.bfloat16)

    def clear(step, carry):
        t_buf[step // 32, step // 8 % 4, step // 2 % 4, step % 2, ROWS:, :] = jnp.zeros((PAD - ROWS, LANES), jnp.bfloat16)
        return carry

    lax.fori_loop(0, CHUNKS * NX * NZ * NK, clear, 0)

    part_a = pl.ds(0, A_ROWS)
    part_b = pl.ds(A_ROWS, ROWS - A_ROWS)

    def copy(src, dst, ssem, rsem, dev):
        return pltpu.make_async_remote_copy(
            src_ref=src, dst_ref=dst, send_sem=ssem, recv_sem=rsem, device_id=dev, device_id_type=MESH
        )

    def same(ref, ssem, rsem, dev):
        return copy(ref, ref, ssem, rsem, dev)

    az_s, ax_s, bx_s, bz_s, sib_s, y_s, z_s, zk_s, x_s = (send_sem.at[i] for i in range(9))

    def az(c, z0, way):
        return same(t_buf.at[c, xx, z0, kk, part_a], az_s, az_r.at[c, z0], zdev(zz + way))

    def bz(c, z0, way):
        return same(t_buf.at[c, :, z0, kk, part_b], bz_s, bz_r.at[c, z0], zdev(zz + way))

    def turn(c, z0):
        return 1 - 2 * ((c + z0) % 2)

    def ax(c, z0, way):
        s = turn(c, z0) if way == 2 else 1 - 2 * way
        source = (xx - s + 4) % 4 if way == 2 else xx
        return same(t_buf.at[c, source, z0, kk, part_a], ax_s, ax_r.at[c, z0, way // 2], xdev((xx + s + 4) % 4))

    def ax_near(c, z0):
        return same(t_buf.at[c, 0:2, z0, kk, part_a], ax_s, ax_r.at[c, z0, 0], sib)

    def ax_far(c, z0):
        return same(t_buf.at[c, (xx + 2) % 4, z0, kk, part_a], ax_s, ax_r.at[c, z0, 1], sib)

    def bx(c, way):
        s = turn(c, 0) if way == 2 else 1 - 2 * way
        source = (xx - s + 4) % 4 if way == 2 else xx
        return same(t_buf.at[c, source, zz, kk, part_b], bx_s, bx_r.at[c, way // 2], xdev((xx + s + 4) % 4))

    def bx_near(c):
        return same(t_buf.at[c, 0:2, zz, kk, part_b], bx_s, bx_r.at[c, 0], sib)

    def bx_far(c):
        return same(t_buf.at[c, (xx + 2) % 4, zz, kk, part_b], bx_s, bx_r.at[c, 1], sib)

    def sb(c, z0):
        return same(t_buf.at[c, :, z0, kk, 0:ROWS], sib_s, sib_r.at[c], sib)

    def sides(distance, act):
        for sign in (-1, 1):
            z0 = zz + sign * distance

            @pl.when((z0 >= 0) & (z0 < NZ))
            def _():
                act(z0, sign)

    def pass_on(sign, send):
        if sign <= 0:

            @pl.when(zz < NZ - 1)
            def _():
                send(1)

        if sign >= 0:

            @pl.when(zz > 0)
            def _():
                send(-1)

    def z_step(c, distance):
        def act(z0, sign):
            az(c, z0, 0).wait_recv()
            pass_on(sign, lambda way: az(c, z0, way).start())
            ax(c, z0, 0).start()
            ax(c, z0, 1).start()

        sides(distance, act)

    def far_step(c, distance):
        def act(z0, sign):
            ax_near(c, z0).wait_recv()
            ax(c, z0, 2).start()

        act(zz, 0) if distance == 0 else sides(distance, act)

    def row_step(c, distance):
        def act(z0, sign):
            if distance == 0:
                bx_far(c).wait_recv()
            else:
                bz(c, z0, 0).wait_recv()
            pass_on(sign, lambda way: bz(c, z0, way).start())
            ax_far(c, z0).wait_recv()
            sb(c, z0).start()

        act(zz, 0) if distance == 0 else sides(distance, act)

    def own_fill(c):
        q = lax.broadcasted_iota(jnp.int32, (1, LANES), 1)
        q_y, q_h, q_z, q_x = q // 32, q // 16 % 2, q // 4 % 4, q % 4
        pair = (q_h * 4 + q_y) * 128 + (q_x * 8 + q_z * 2 + c % 2) * 4 + c // 2
        pick = lax.broadcasted_iota(jnp.int32, (tau_ref.shape[1], LANES), 0) == pair
        block = jnp.dot(
            w_buf[...], pick.astype(jnp.float32).astype(jnp.bfloat16), preferred_element_type=jnp.float32
        )
        t_buf[c, xx, zz, kk, 0:ROWS, :] = block.astype(jnp.bfloat16)

    def own_send(c):
        pass_on(0, lambda way: az(c, zz, way).start())
        bx(c, 0).start()
        bx(c, 1).start()
        ax(c, zz, 0).start()
        ax(c, zz, 1).start()

    def bx_step(c):
        bx_near(c).wait_recv()
        bx(c, 2).start()

    def turn_v(step):
        def one(i, carry):
            t = step * 8 + i
            first = pl.multiple_of((kpiece * t) // 16 * 16, 16)
            lanes = pl.ds(pl.multiple_of(t * PAD, PAD), PAD)
            for s in range(v_buf.shape[0]):
                vt_buf[s * 128 : (s + 1) * 128, lanes] = v_buf[s, pl.ds(first, PAD), :].T
            return carry

        lax.fori_loop(0, 8, one, 0)

    def multiply(c, x):
        block = t_buf[c, x].reshape(NZ * NK * PAD, LANES)
        product = jnp.dot(
            vt_buf[:, x * NZ * NK * PAD : (x + 1) * NZ * NK * PAD], block, preferred_element_type=jnp.float32
        )
        if x == 0:
            acc[...] = product
        else:
            acc[...] += product

    def y_out(c, step):
        other = (yy + step) % NY
        rows = pl.ds(pl.multiple_of(other * 32, 32), 32)
        return copy(r_buf.at[c, rows], y_buf.at[c, 3 - step], y_s, y_r.at[c], ydev(other))

    def y_step(c):
        for s in range(v_buf.shape[0]):
            r_buf[c, :, s * 128 : (s + 1) * 128] = (acc[s * 128 : (s + 1) * 128, :] * scales_ref[s]).T
        for step in (2, 1, 3):
            y_out(c, step).start()

    def z_out(c, place, sem):
        mine = (hh * NZ + zz) * NK + kk
        return copy(
            q_buf.at[c, place], z_buf.at[c // 2, mine], sem, z_r.at[c // 2], ring(place // NZ, place % NZ, c % 2)
        )

    def zs_step(c):
        same(y_buf.at[c], y_s, y_r.at[c], sib).wait_recv()
        mine = r_buf[c, pl.ds(pl.multiple_of(yy * 32, 32), 32), :]
        total = mine + y_buf[c, 0] + y_buf[c, 1] + y_buf[c, 2]
        for place in range(NH * NZ):
            q_buf[c, place] = total[place * 4 : place * 4 + 4, :]

        @pl.when(kk == c % 2)
        def _():
            z_buf[c // 2, (hh * NZ + zz) * NK + kk] = q_buf[c, hh * NZ + zz]

        @pl.when(kk != c % 2)
        def _():
            z_out(c, hh * NZ + zz, zk_s).start()

        def one(step, carry):
            z_out(c, (hh * NZ + zz + step) % (NH * NZ), z_s).start()
            return carry

        lax.fori_loop(1, NH * NZ, one, 0)

    def x_out(j, step):
        other = (xx + step) % NX
        return copy(s_buf.at[j, other], out_ref.at[j, xx], x_s, x_r, xdev(other))

    def xs_step(c):
        j = c // 2

        @pl.when(kk == c % 2)
        def _():
            received = z_buf.at[j, 0 : NH * NZ * NK - 1]
            same(received, z_s, z_r.at[j], sib).wait_recv()
            for source in range(NZ * NK):
                both = z_buf[j, source] + z_buf[j, NZ * NK + source]
                for x in range(NX):
                    s_buf[j, x, source : source + 1, :] = both[x : x + 1, :]
            for step in (2, 1, 3):
                x_out(j, step).start()
            out_ref[j, xx] = s_buf[j, xx]

    def when_in(c, act):
        @pl.when((c >= 0) & (c < CHUNKS))
        def _():
            act()

    own_fill(0)
    own_fill(1)
    pl.semaphore_wait(barrier, (NX - 1) + (NY - 1) + 1 + (NH * NZ - 1) * NK)
    own_send(0)

    def tick(tau, carry):
        when_in(tau + 1, lambda: own_send(tau + 1))
        c = tau - 6
        when_in(c, lambda: same(t_buf.at[c, :, :, 1 - kk, 0:ROWS], sib_s, sib_r.at[c], sib).wait_recv())
        when_in(tau - 1, lambda: (bx_step(tau - 1), z_step(tau - 1, 1), far_step(tau - 1, 0)))
        when_in(c, lambda: multiply(c, 0))
        when_in(tau - 2, lambda: (row_step(tau - 2, 0), far_step(tau - 2, 1), z_step(tau - 2, 2)))
        when_in(c, lambda: multiply(c, 1))
        when_in(tau - 3, lambda: (row_step(tau - 3, 1), far_step(tau - 3, 2), z_step(tau - 3, 3)))
        when_in(c, lambda: multiply(c, 2))
        when_in(tau - 4, lambda: (row_step(tau - 4, 2), far_step(tau - 4, 3)))
        when_in(c, lambda: multiply(c, 3))
        when_in(tau - 5, lambda: row_step(tau - 5, 3))
        when_in(c, lambda: y_step(c))
        when_in(tau - 7, lambda: zs_step(tau - 7))
        when_in(tau - 8, lambda: xs_step(tau - 8))

        @pl.when(tau == 0)
        def _():
            v_copy.wait()

        @pl.when(tau < 4)
        def _():
            turn_v(tau)

        when_in(tau + 2, lambda: own_fill(tau + 2))
        return carry

    lax.fori_loop(0, CHUNKS + 8, tick, 0)

    def sent(ref, sem):
        same(ref, sem, sem, sib).wait_send()

    sent(t_buf.at[:, 0:3, :, 0, part_a], ax_s)
    sent(t_buf.at[:, 0:3, 0, 0, part_b], bx_s)
    sent(t_buf.at[:, :, :, 0, 0:ROWS], sib_s)

    @pl.when((zz == 0) | (zz == NZ - 1))
    def _():
        sent(t_buf.at[:, 0, 0, 0, part_a], az_s)
        sent(t_buf.at[:, :, 0, 0, part_b], bz_s)

    @pl.when((zz > 0) & (zz < NZ - 1))
    def _():
        sent(t_buf.at[0:5, 0:2, :, 0, part_a], az_s)
        sent(t_buf.at[0:5, :, :, :, part_b], bz_s)

    sent(r_buf.at[:, 0:96], y_s)
    sent(q_buf.at[:, 0 : NH * NZ - 1], z_s)
    sent(q_buf.at[0 : CHUNKS // 2, 0], zk_s)
    sent(s_buf.at[:, 0 : NX - 1], x_s)
    same(out_ref.at[:, 0 : NX - 1], x_s, x_r, sib).wait_recv()


def local(tau, vvvv, scales, tile_ids, counts, spin_c, spin_d, pair_energy, ab_energy):
    slots, width, klayer = vvvv.shape
    pairs, kpiece = tau.shape
    ntile = lax.axis_size("tile")
    nlayer = lax.axis_size("layer")
    own_pairs = pairs // (nlayer * ntile)
    all_slots = slots * ntile
    vmem = pl.BlockSpec(memory_space=pltpu.VMEM)
    bf16, f32 = jnp.bfloat16, jnp.float32
    dma = pltpu.SemaphoreType.DMA
    owned = pl.pallas_call(
        ladder_kernel,
        out_shape=jax.ShapeDtypeStruct((own_pairs, NX, NZ * NK, slots * width), f32),
        in_specs=[vmem, pl.BlockSpec(memory_space=pl.ANY), pl.BlockSpec(memory_space=pltpu.SMEM), vmem, vmem],
        out_specs=vmem,
        scratch_shapes=[
            pltpu.VMEM((CHUNKS, NX, NZ, NK, PAD, LANES), bf16),
            pltpu.VMEM((slots, klayer + 16, width), bf16),
            pltpu.VMEM((slots * width, ntile * PAD), bf16),
            pltpu.VMEM((ROWS, pairs), bf16),
            pltpu.VMEM((slots * width, LANES), f32),
            pltpu.VMEM((CHUNKS, LANES, slots * width), f32),
            pltpu.VMEM((CHUNKS, NY - 1, LANES // NY, slots * width), f32),
            pltpu.VMEM((CHUNKS, NH * NZ, NX, slots * width), f32),
            pltpu.VMEM((own_pairs, NH * NZ * NK, NX, slots * width), f32),
            pltpu.VMEM((own_pairs, NX, NZ * NK, slots * width), f32),
            dma,
            dma((9,)),
            dma((CHUNKS, NZ)),
            dma((CHUNKS, NZ, 2)),
            dma((CHUNKS, 2)),
            dma((CHUNKS, NZ)),
            dma((CHUNKS,)),
            dma((CHUNKS,)),
            dma((own_pairs,)),
            dma,
        ],
        compiler_params=pltpu.CompilerParams(
            collective_id=0, has_side_effects=True, vmem_limit_bytes=56 * 1024 * 1024
        ),
        name="ladder",
    )(tau.T, jnp.swapaxes(vvvv, 1, 2), scales, spin_c[None, :], spin_d[None, :])
    slot_index = jnp.arange(all_slots, dtype=jnp.int32)
    owner = slot_index // slots
    owner_count = jnp.sum(
        jnp.where(owner[:, None] == jnp.arange(ntile, dtype=jnp.int32)[None, :], counts[None, :], 0), axis=1
    )
    valid = slot_index % slots < owner_count
    onehot = ((tile_ids[:, None] == slot_index[None, :]) & valid[:, None]).astype(jnp.float32)
    residual = jnp.einsum(
        "pga,gj->pja",
        owned.reshape(own_pairs, all_slots, width),
        onehot,
        precision=lax.Precision.HIGHEST,
    )
    denom = ab_energy[None, :, :] - pair_energy[:, None, None]
    return (residual / denom).reshape(own_pairs, all_slots * width)


def solution(mesh):
    placed = (
        P(None, ("layer", "tile")),
        P("tile", None, "layer"),
        P("tile"),
        P(),
        P(),
        P(),
        P(),
        P(("layer", "tile")),
        P(),
    )
    return jax.shard_map(
        local, mesh=mesh, in_specs=placed, out_specs=P(("layer", "tile"), None), check_vma=False
    )
```

time: 143 us -> 107 us (0.75)
  Pallas kernels: 138 us -> 102 us
    pallas_call x1, Pallas kernels: 138 us -> 102 us  [local(): pl.pallas_call(ladder_kernel, out_shape=jax.ShapeDtypeStruct((own_pairs,...]
where the time goes in v2:
time: 107 us; the launch traced here: 106 us
  Pallas kernels  102 us (95%)
  local copies, waits for them, and re-layouts  3.15 us (3%)
    pallas_call x1, Pallas kernels, local(): pl.pallas_call(ladder_kernel, out_shape=jax.ShapeDtypeStruct((own_pairs,...  102 us

profile of v2, /device:TPU:1, one launch (start us, length us, event | category | flops | bytes accessed | tf_op | source)
XLA Modules:
  0.0 106.5 jit_solution(4166405311894428219)
XLA Ops:
  0.0 0.0 copy-start
  0.0 0.0 copy-start.1
  0.0 0.0 copy-start.2
  0.0 0.8 select_reduce_fusion
  0.8 1.3 %broadcast_in_dim.29.spin_d_ref = s32[1,1200]{1,0:T(1,128)} reshape(s32[1200]{0:T(1024)} %param.15) | data formatting | bytes 9600 | tf_op jit(solution)/shard_map/broadcast_in_dim | solution.py:420
  2.1 102.2 %ladder.1 = f32[4,4,8,512]{3,2,1,0:T(8,128)} custom-call(bf16[225,1024]{1,0:T(8,128)(2,1)} %bitcast.21, bf16[4,7200,128]{2,1,0:T(8,128)(2,1)} %bitcast.20, f32[4]{0:T(128)} %scales_ref.1, s32[1,48]{1,0:T(1,128)} %bitcast.22, s32[1,1200]{1,0:T(1,128)} %broadcast_in_dim.29.spin_d_ref), custom_call_target="tpu_custom_call" | custom-call | tf_op jit(solution)/shard_map/ladder/pallas_call | solution.py:389
  104.3 1.0 reshape.35
  105.3 0.0 copy-done
  105.3 0.0 copy-done.1
  105.3 0.0 copy-done.2
  105.3 0.3 fusion.1
  105.6 0.9 copy.12
  (2 shorter events, 0.0 us)
Async XLA Ops:
  0.0 105.3 %copy-start = (f32[128,128]{1,0:T(8,128)S(1)}, f32[128,128]{1,0:T(8,128)}, u32[]{:S(2)}) copy-start(f32[128,128]{1,0:T(8,128)} %param.17) | copy-start | bytes 196612
  0.0 105.3 %copy-start.1 = (f32[4]{0:T(128)S(1)}, f32[4]{0:T(128)}, u32[]{:S(2)}) copy-start(f32[4]{0:T(128)} %param.16) | copy-start | bytes 52
  0.0 105.3 %copy-start.2 = (s32[128]{0:T(128)S(1)}, s32[128]{0:T(128)}, u32[]{:S(2)}) copy-start(s32[128]{0:T(128)} %param.12) | copy-start | bytes 1540

commit v3 on v0

v3 whole, which is shorter than its diff:
```python
import functools

import jax
import jax.numpy as jnp
from jax import lax
from jax.experimental import pallas as pl
from jax.experimental.pallas import tpu as pltpu
from jax.sharding import PartitionSpec as P

MESH = pl.DeviceIdType.MESH

NX, NZ, NK, NY, NH = 4, 4, 2, 4, 2
UNITS = ((3, (0,)), (0, (0, 1)), (1, (0, 1)), (2, (0, 1)), (3, (1,)))
LANES = tuple(128 * len(cores) for _, cores in UNITS)
COUNT = len(UNITS)
ROWS = 240
PAD = 256
A_ROWS = 176


def ladder_kernel(
    tau_ref,
    v_hbm,
    scales_ref,
    spin_c_ref,
    spin_d_ref,
    ids_ref,
    counts_ref,
    pair_ref,
    ab_ref,
    out_ref,
    own_buf,
    pick_buf,
    t_bufs,
    v_buf,
    vt_buf,
    w_buf,
    accs,
    r_bufs,
    y_bufs,
    q_bufs,
    z_bufs,
    s_buf,
    v_sem,
    send_sem,
    x_s,
    az_r,
    ax_r,
    bx_r,
    bz_r,
    sib_r,
    y_r,
    z_r,
    x_r,
):
    layer = lax.axis_index("layer")
    tile = lax.axis_index("tile")
    xx, zz, kk = tile // 8, (tile // 2) % 4, tile % 2
    hh, yy = layer // 4, layer % 4
    kpiece = tau_ref.shape[0]
    klayer = v_hbm.shape[1]
    virtual = spin_d_ref.shape[0]
    panel = spin_c_ref.shape[0]

    place = hh * NZ + zz

    def xdev(x, core=None):
        return (layer, x * 8 + zz * 2 + (kk if core is None else core))

    def zdev(z):
        return (layer, xx * 8 + z * 2 + kk)

    sib = xdev(xx, 1 - kk)

    def ydev(y):
        return (hh * 4 + y, tile)

    def ring(other):
        return (other // NZ * 4 + yy, xx * 8 + other % NZ * 2 + kk)

    barrier = pltpu.get_barrier_semaphore()

    def greet(dev):
        pl.semaphore_signal(barrier, inc=1, device_id=dev, device_id_type=MESH)

    for step in range(1, NH * NZ):
        greet(ring((place + step) % (NH * NZ)))
    for step in range(1, NX):
        greet(xdev((xx + step) % NX))
    for step in range(1, NY):
        greet(ydev((yy + step) % NY))
    for step in range(NX):
        greet(xdev((xx + step) % NX, 1 - kk))

    v_copy = pltpu.make_async_copy(v_hbm, v_buf.at[:, pl.ds(0, klayer)], v_sem)
    v_copy.start()
    v_buf[:, klayer:, :] = jnp.zeros((v_buf.shape[0], v_buf.shape[1] - klayer, 128), v_buf.dtype)

    start = (kpiece * tile) // 16 * 16
    offset = kpiece * tile - start
    base = layer * klayer + start
    c_first = base // virtual
    d_first = base - c_first * virtual
    row = lax.broadcasted_iota(jnp.int32, (ROWS, 1), 0)
    d_index = row + d_first
    over = d_index >= virtual
    d_index = jnp.where(over, d_index - virtual, d_index)
    c_index = jnp.where(over, c_first + 1, c_first)
    d_iota = lax.broadcasted_iota(jnp.int32, (ROWS, virtual), 1)
    c_iota = lax.broadcasted_iota(jnp.int32, (ROWS, panel), 1)
    spin_right = jnp.sum(jnp.where(d_iota == d_index, spin_d_ref[...][None, :], 0).astype(jnp.float32), axis=1, keepdims=True)
    spin_left = jnp.sum(jnp.where(c_iota == c_index, spin_c_ref[...][None, :], 0).astype(jnp.float32), axis=1, keepdims=True)
    factor = jnp.where(spin_left == spin_right, 0.5, 1.0)
    shift = (
        lax.broadcasted_iota(jnp.int32, (ROWS, kpiece), 0) - offset
        == lax.broadcasted_iota(jnp.int32, (ROWS, kpiece), 1)
    )
    placed = jnp.dot(
        shift.astype(jnp.float32).astype(jnp.bfloat16), tau_ref[...], preferred_element_type=jnp.float32
    )
    w_buf[...] = (placed * factor).astype(jnp.bfloat16)

    def clear(step, carry):
        for t_buf in t_bufs:
            t_buf[step // 8, step // 2 % 4, step % 2, ROWS:, :] = jnp.zeros((PAD - ROWS, t_buf.shape[-1]), jnp.bfloat16)
        return carry

    lax.fori_loop(0, NX * NZ * NK, clear, 0)

    part_a = pl.ds(0, A_ROWS)
    part_b = pl.ds(A_ROWS, ROWS - A_ROWS)

    def copy(src, dst, ssem, rsem, dev):
        return pltpu.make_async_remote_copy(
            src_ref=src, dst_ref=dst, send_sem=ssem, recv_sem=rsem, device_id=dev, device_id_type=MESH
        )

    def same(ref, ssem, rsem, dev):
        return copy(ref, ref, ssem, rsem, dev)

    def kind(u, i):
        return send_sem.at[u, i]

    def az(u, z0, way):
        return same(t_bufs[u].at[z0, xx, kk, part_a], kind(u, 0 if way > 0 else 7), az_r.at[u, z0], zdev(zz + way))

    def bz(u, z0, way):
        return same(t_bufs[u].at[z0, :, kk, part_b], kind(u, 1 if way > 0 else 8), bz_r.at[u, z0], zdev(zz + way))

    def turn(u, z0):
        return 1 - 2 * ((u + z0) % 2)

    def ax(u, z0, way):
        s = turn(u, z0) if way == 2 else 1 - 2 * way
        source = (xx - s + 4) % 4 if way == 2 else xx
        return same(t_bufs[u].at[z0, source, kk, part_a], kind(u, 2), ax_r.at[u, z0, way // 2], xdev((xx + s + 4) % 4))

    def ax_near(u, z0):
        return same(t_bufs[u].at[z0, 0:2, kk, part_a], kind(u, 2), ax_r.at[u, z0, 0], sib)

    def ax_far(u, z0):
        return same(t_bufs[u].at[z0, (xx + 2) % 4, kk, part_a], kind(u, 2), ax_r.at[u, z0, 1], sib)

    def bx(u, way):
        s = turn(u, 0) if way == 2 else 1 - 2 * way
        source = (xx - s + 4) % 4 if way == 2 else xx
        return same(t_bufs[u].at[zz, source, kk, part_b], kind(u, 3), bx_r.at[u, way // 2], xdev((xx + s + 4) % 4))

    def bx_near(u):
        return same(t_bufs[u].at[zz, 0:2, kk, part_b], kind(u, 3), bx_r.at[u, 0], sib)

    def bx_far(u):
        return same(t_bufs[u].at[zz, (xx + 2) % 4, kk, part_b], kind(u, 3), bx_r.at[u, 1], sib)

    def sb(u, z0):
        return same(t_bufs[u].at[z0, :, kk, 0:ROWS], kind(u, 4), sib_r.at[u, z0], sib)

    def sides(distance, act):
        for sign in (-1, 1):
            z0 = zz + sign * distance

            @pl.when((z0 >= 0) & (z0 < NZ))
            def _():
                act(z0, sign)

    def pass_on(sign, send):
        if sign <= 0:

            @pl.when(zz < NZ - 1)
            def _():
                send(1)

        if sign >= 0:

            @pl.when(zz > 0)
            def _():
                send(-1)

    def rows_at(distance, act):
        act(zz, 0) if distance == 0 else sides(distance, act)

    def z_step(u, distance):
        def act(z0, sign):
            az(u, z0, 0).wait_recv()
            pass_on(sign, lambda way: az(u, z0, way).start())
            ax(u, z0, 0).start()
            ax(u, z0, 1).start()

        sides(distance, act)

    def far_step(u, distance):
        def act(z0, sign):
            ax_near(u, z0).wait_recv()
            ax(u, z0, 2).start()

        rows_at(distance, act)

    def row_step(u, distance):
        def act(z0, sign):
            if distance == 0:
                bx_far(u).wait_recv()
            else:
                bz(u, z0, 0).wait_recv()
            pass_on(sign, lambda way: bz(u, z0, way).start())
            ax_far(u, z0).wait_recv()
            sb(u, z0).start()

        rows_at(distance, act)

    def own_fill(u):
        j, cores = UNITS[u]
        n, lanes = len(cores), LANES[u]
        q = lax.broadcasted_iota(jnp.int32, (1, lanes), 1)
        q_y, q_h, q_z, q_k, q_x = q // (32 * n), q // (16 * n) % 2, q // (4 * n) % 4, q // 4 % n + cores[0], q % 4
        pair = (q_h * 4 + q_y) * 128 + (q_x * 8 + q_z * 2 + q_k) * 4 + j
        pick = lax.broadcasted_iota(jnp.int32, (tau_ref.shape[1], lanes), 0) == pair
        block = jnp.dot(
            w_buf[...], pick.astype(jnp.float32).astype(jnp.bfloat16), preferred_element_type=jnp.float32
        )
        t_bufs[u][zz, xx, kk, 0:ROWS, :] = block.astype(jnp.bfloat16)

    def own_send(u):
        pass_on(0, lambda way: az(u, zz, way).start())
        bx(u, 0).start()
        bx(u, 1).start()
        ax(u, zz, 0).start()
        ax(u, zz, 1).start()

    def bx_step(u):
        bx_near(u).wait_recv()
        bx(u, 2).start()

    def turn_v(step):
        def one(i, carry):
            t = step * 16 + i
            first = pl.multiple_of((kpiece * t) // 16 * 16, 16)
            block = (t // 2 % NZ * NX + t // 8) * NK + t % NK
            lanes = pl.ds(pl.multiple_of(block * PAD, PAD), PAD)
            for s in range(v_buf.shape[0]):
                vt_buf[s * 128 : (s + 1) * 128, lanes] = v_buf[s, pl.ds(first, PAD), :].T
            return carry

        lax.fori_loop(0, 16, one, 0)

    def multiply(u, distance):
        depth = NX * NK * PAD

        def act(z0, sign):
            t_bufs_row = t_bufs[u].at[z0]
            same(t_bufs_row.at[:, 1 - kk, 0:ROWS], kind(u, 4), sib_r.at[u, z0], sib).wait_recv()
            if distance == 0:
                accs[u][...] = jnp.zeros(accs[u].shape, jnp.float32)

            def one(i, carry):
                size = depth // 2
                part = vt_buf[:, pl.ds(pl.multiple_of(z0 * depth + i * size, size), size)]
                block = t_bufs_row[pl.ds(i * 2, 2)].reshape(size, LANES[u])
                accs[u][...] += jnp.dot(part, block, preferred_element_type=jnp.float32)
                return carry

            lax.fori_loop(0, 2, one, 0)

        rows_at(distance, act)

    def y_step(u):
        r_buf = r_bufs[u]
        quarter = r_buf.shape[0] // NY
        for half in range(LANES[u] // 128):
            lanes = slice(half * 128, half * 128 + 128)
            for s in range(v_buf.shape[0]):
                rows = slice(s * 128, s * 128 + 128)
                r_buf[lanes, rows] = (accs[u][rows, lanes] * scales_ref[s]).T
        for step in (2, 1, 3):
            other = (yy + step) % NY
            rows = pl.ds(pl.multiple_of(other * quarter, quarter), quarter)
            copy(r_buf.at[rows], y_bufs[u].at[3 - step], kind(u, 5), y_r.at[u], ydev(other)).start()

    def zs_step(u):
        r_buf, y_buf, q_buf, z_buf = r_bufs[u], y_bufs[u], q_bufs[u], z_bufs[u]
        quarter = r_buf.shape[0] // NY
        rows = q_buf.shape[1]
        same(y_buf, kind(u, 5), y_r.at[u], sib).wait_recv()
        mine = r_buf[pl.ds(pl.multiple_of(yy * quarter, quarter), quarter), :]
        total = mine + y_buf[0] + y_buf[1] + y_buf[2]
        for other in range(NH * NZ):
            q_buf[other] = total[other * rows : (other + 1) * rows, :]
        z_buf[place] = q_buf[place]
        for step in (4, 3, 5, 2, 6, 1, 7):
            other = (place + step) % (NH * NZ)
            copy(q_buf.at[other], z_buf.at[place], kind(u, 6), z_r.at[u], ring(other)).start()

    def xs_step(u):
        z_buf = z_bufs[u]
        j, cores = UNITS[u]
        same(z_buf.at[0 : NH * NZ - 1], kind(u, 6), z_r.at[u], sib).wait_recv()
        for z in range(NZ):
            both = z_buf[z] + z_buf[NZ + z]
            for i, core in enumerate(cores):
                for x in range(NX):
                    s_buf[j, core * NX + x, z : z + 1, :] = both[i * NX + x : i * NX + x + 1, :]

        def send(core, step):
            other = (xx + step) % NX
            copy(s_buf.at[j, core * NX + other], own_buf.at[j, xx * NK + kk], x_s, x_r, xdev(other, core)).start()

        for core in cores:

            @pl.when(kk == core)
            def _():
                for step in (2, 1, 3):
                    send(core, step)
                own_buf[j, xx * NK + kk] = s_buf[j, core * NX + xx]

            @pl.when(kk != core)
            def _():
                for step in (2, 1, 3, 0):
                    send(core, step)

    def sent(ref, sem):
        same(ref, sem, sem, sib).wait_send()

    def gather_sent(u):
        t_buf = t_bufs[u]
        sent(t_buf.at[0:3, :, 0, part_a], kind(u, 2))
        sent(t_buf.at[0:3, 0, 0, part_b], kind(u, 3))
        sent(t_buf.at[:, :, 0, 0:ROWS], kind(u, 4))

        for v in range(NZ):

            @pl.when(zz == v)
            def _():
                for count, i in ((v + 1 if v < NZ - 1 else 0, 0), (NZ - v if v > 0 else 0, 7)):
                    if count:
                        sent(t_buf.at[0, 0:count, 0, part_a], kind(u, i))
                        sent(t_buf.at[:, 0:count, 0, part_b], kind(u, i + 1))

    def slot_pick():
        slots, owners = v_buf.shape[0], NX * NK * NZ
        g = lax.broadcasted_iota(jnp.int32, (owners, slots * owners), 1)
        t = lax.broadcasted_iota(jnp.int32, (owners, slots * owners), 0)
        held = jnp.where(g // slots == t, 1.0, 0.0).astype(jnp.bfloat16)
        counts = jnp.broadcast_to(counts_ref[...][None, :], (8, owners)).astype(jnp.float32).astype(jnp.bfloat16)
        count = jnp.dot(counts, held, preferred_element_type=jnp.float32)
        ids = jnp.broadcast_to(ids_ref[...][None, :], count.shape).astype(jnp.float32)
        slot = lax.broadcasted_iota(jnp.int32, count.shape, 1) % slots
        ids = jnp.where(slot.astype(jnp.float32) < count, ids, -1.0).astype(jnp.bfloat16)
        g = lax.broadcasted_iota(jnp.int32, (slots * owners, owners), 0)
        r = lax.broadcasted_iota(jnp.int32, (slots * owners, owners), 1)
        t = r // (NK * NZ) * (NK * NZ) + r % NZ * NK + r // NZ % NK
        j = lax.broadcasted_iota(jnp.int32, (slots * owners, owners), 0).astype(jnp.float32)
        for s in range(slots):
            order = jnp.where(g == t * slots + s, 1.0, 0.0).astype(jnp.bfloat16)
            mine = jnp.dot(ids, order, preferred_element_type=jnp.float32)
            pick_buf[s] = jnp.where(mine[0:1, :] == j, 1.0, 0.0)

    own_fill(0)
    own_fill(1)
    slot_pick()
    pl.semaphore_wait(barrier, (NX - 1) + (NY - 1) + (NH * NZ - 1) + NX)
    own_send(0)

    for tick in range(COUNT + 8):

        def at(stage, act):
            if 0 <= tick - stage < COUNT:
                act(tick - stage)

        at(-1, own_send)
        at(1, lambda u: (bx_step(u), z_step(u, 1), far_step(u, 0)))
        at(3, lambda u: multiply(u, 0))
        at(2, lambda u: (row_step(u, 0), far_step(u, 1), z_step(u, 2)))
        at(4, lambda u: multiply(u, 1))
        at(3, lambda u: (row_step(u, 1), far_step(u, 2), z_step(u, 3)))
        at(5, lambda u: multiply(u, 2))
        at(4, lambda u: (row_step(u, 2), far_step(u, 3)))
        at(5, lambda u: row_step(u, 3))
        at(6, lambda u: multiply(u, 3))
        at(6, y_step)
        at(7, zs_step)
        at(8, xs_step)
        if tick == 0:
            v_copy.wait()
        if tick < 2:
            turn_v(tick)
        at(-2, own_fill)
        at(6, gather_sent)

    for u in range(COUNT):
        sent(r_bufs[u].at[0 : r_bufs[u].shape[0] // 4 * 3], kind(u, 5))
        sent(q_bufs[u].at[0 : NH * NZ - 1], kind(u, 6))
    sent(s_buf.at[:, 0 : NX * NK - 1], x_s)
    same(own_buf.at[:, 0 : NX * NK - 1], x_s, x_r, sib).wait_recv()
    width = ab_ref.shape[1]
    for p in range(own_buf.shape[0]):
        owned = own_buf[p].reshape(NX * NK * NZ, own_buf.shape[3])
        residual = jnp.zeros(ab_ref.shape, jnp.float32)
        for s in range(v_buf.shape[0]):
            residual += jnp.dot(
                pick_buf[s],
                owned[:, s * width : (s + 1) * width],
                precision=lax.Precision.HIGHEST,
                preferred_element_type=jnp.float32,
            )
        out_ref[:, p, :] = residual / (ab_ref[...] - pair_ref[p])


def local(tau, vvvv, scales, tile_ids, counts, spin_c, spin_d, pair_energy, ab_energy):
    slots, width, klayer = vvvv.shape
    pairs, kpiece = tau.shape
    ntile = lax.axis_size("tile")
    nlayer = lax.axis_size("layer")
    own_pairs = pairs // (nlayer * ntile)
    all_slots = slots * ntile
    vmem = pl.BlockSpec(memory_space=pltpu.VMEM)
    bf16, f32 = jnp.bfloat16, jnp.float32
    dma = pltpu.SemaphoreType.DMA
    columns = slots * width
    smem = pl.BlockSpec(memory_space=pltpu.SMEM)
    amplitudes = pl.pallas_call(
        ladder_kernel,
        out_shape=jax.ShapeDtypeStruct((all_slots, own_pairs, width), f32),
        in_specs=[vmem, pl.BlockSpec(memory_space=pl.ANY), smem, vmem, vmem, vmem, vmem, smem, vmem],
        out_specs=vmem,
        scratch_shapes=[
            pltpu.VMEM((own_pairs, NX * NK, NZ, columns), f32),
            pltpu.VMEM((slots, all_slots, ntile), f32),
            [pltpu.VMEM((NZ, NX, NK, PAD, lanes), bf16) for lanes in LANES],
            pltpu.VMEM((slots, klayer + 16, width), bf16),
            pltpu.VMEM((columns, ntile * PAD), bf16),
            pltpu.VMEM((ROWS, pairs), bf16),
            [pltpu.VMEM((columns, lanes), f32) for lanes in LANES],
            [pltpu.VMEM((lanes, columns), f32) for lanes in LANES],
            [pltpu.VMEM((NY - 1, lanes // NY, columns), f32) for lanes in LANES],
            [pltpu.VMEM((NH * NZ, lanes // 32, columns), f32) for lanes in LANES],
            [pltpu.VMEM((NH * NZ, lanes // 32, columns), f32) for lanes in LANES],
            pltpu.VMEM((own_pairs, NX * NK, NZ, columns), f32),
            dma,
            dma((COUNT, 9)),
            dma,
            dma((COUNT, NZ)),
            dma((COUNT, NZ, 2)),
            dma((COUNT, 2)),
            dma((COUNT, NZ)),
            dma((COUNT, NZ)),
            dma((COUNT,)),
            dma((COUNT,)),
            dma,
        ],
        compiler_params=pltpu.CompilerParams(
            collective_id=0, has_side_effects=True, vmem_limit_bytes=56 * 1024 * 1024
        ),
        name="ladder",
    )(tau.T, jnp.swapaxes(vvvv, 1, 2), scales, spin_c, spin_d, tile_ids, counts, pair_energy, ab_energy)
    return jnp.swapaxes(amplitudes, 0, 1).reshape(own_pairs, all_slots * width)


def solution(mesh):
    placed = (
        P(None, ("layer", "tile")),
        P("tile", None, "layer"),
        P("tile"),
        P(),
        P(),
        P(),
        P(),
        P(("layer", "tile")),
        P(),
    )
    return jax.shard_map(
        local, mesh=mesh, in_specs=placed, out_specs=P(("layer", "tile"), None), check_vma=False
    )
```

time: 256 us -> 103 us (0.40)
  waiting for transfers between devices: 202 us -> 0 us
  Pallas kernels: 0 us -> 101 us
  local copies, waits for them, and re-layouts: 16.6 us -> 1.67 us
  matrix products: 13.8 us -> 0 us
  between operations: 13.5 us -> 0.01 us
  starting transfers between devices: 6.59 us -> 0 us
  other arithmetic: 3.78 us -> 0 us
    pallas_call x0 -> x1, Pallas kernels: none -> 101 us  [local(): pl.pallas_call(ladder_kernel, out_shape=jax.ShapeDtypeStruct((all_slots,...]
    all_gather x1 -> x0, waiting for transfers between devices: 96.1 us -> none  [local(): lax.all_gather(weighted, 'tile', axis=1, tiled=True)]
    reduce_scatter x1 -> x0, waiting for transfers between devices: 94.5 us -> none  [local(): reduced = lax.psum_scatter(flat, 'layer', scatter_dimension=0, tiled=True)]
    dot_general x2 -> x0, matrix products: 13.8 us -> none  [the longest x1 13.5 us: local(): jnp.einsum('pk,stk->pst', lax.all_gather(weighted, 'tile', axis=1, tiled=...]
    unnamed x12 -> x1, local copies, waits for them, and re-layouts: 12.9 us -> 1.67 us
    all_to_all x1 -> x0, waiting for transfers between devices: 11.2 us -> none  [local(): lax.all_to_all(reduced, 'tile', split_axis=0, concat_axis=1, tiled=True)]
    all_to_all x1 -> x0, starting transfers between devices: 6.55 us -> none  [local(): lax.all_to_all(reduced, 'tile', split_axis=0, concat_axis=1, tiled=True)]
  transfers between devices with their start and end apart: 3 -> 0, of which waited for: 3 -> 0; matrix products, arithmetic and copies ran while one was open for 0% -> 0% of each run, Pallas kernels for 0% -> 0%
where the time goes in v3:
time: 103 us; the launch traced here: 102 us
  Pallas kernels  101 us (98%)
  local copies, waits for them, and re-layouts  1.67 us (2%)
    pallas_call x1, Pallas kernels, local(): pl.pallas_call(ladder_kernel, out_shape=jax.ShapeDtypeStruct((all_slots,...  101 us

profile of v3, /device:TPU:1, one launch (start us, length us, event | category | flops | bytes accessed | tf_op | source)
XLA Modules:
  0.0 102.4 jit_solution(14531941390336246278)
XLA Ops:
  0.0 100.7 %ladder.1 = f32[128,4,128]{2,1,0:T(4,128)} custom-call(bf16[225,1024]{1,0:T(8,128)(2,1)} %bitcast.7, bf16[4,7200,128]{2,1,0:T(8,128)(2,1)} %bitcast.5, f32[4]{0:T(128)} %scales_ref.1, s32[48]{0:T(128)} %spin_c_ref.1, s32[1200]{0:T(1024)} %spin_d_ref.1, s32[128]{0:T(128)} %ids_ref.1, s32[32]{0:T(128)} %counts_ref.1, f32[4]{0:T(128)} %pair_ref.1, ...), custom_call_target="tpu_custom_call" | custom-call | tf_op jit(solution)/shard_map/ladder/pallas_call | solution.py:439
  100.7 1.7 %copy.11 = f32[4,16384]{1,0:T(4,128)} copy(f32[4,16384]{1,0:T(4,128)} %bitcast.6) | data formatting | bytes 524288

commit v4 on v3

--- a/solution.py
+++ b/solution.py
@@ -13,7 +13,9 @@
 UNITS = ((3, (0,)), (0, (0, 1)), (1, (0, 1)), (2, (0, 1)), (3, (1,)))
 LANES = tuple(128 * len(cores) for _, cores in UNITS)
 COUNT = len(UNITS)
+LAST = COUNT - 1
 ROWS = 240
+FEW = 224
 PAD = 256
 A_ROWS = 176
 
@@ -35,6 +37,7 @@
     v_buf,
     vt_buf,
     w_buf,
+    edge_buf,
     accs,
     r_bufs,
     y_bufs,
@@ -42,8 +45,8 @@
     z_bufs,
     s_buf,
     v_sem,
+    edge_sem,
     send_sem,
-    x_s,
     az_r,
     ax_r,
     bx_r,
@@ -75,8 +78,11 @@
     def ydev(y):
         return (hh * 4 + y, tile)
 
-    def ring(other):
-        return (other // NZ * 4 + yy, xx * 8 + other % NZ * 2 + kk)
+    def ring(other, core=None):
+        return (other // NZ * 4 + yy, xx * 8 + other % NZ * 2 + (kk if core is None else core))
+
+    def plane(y, x):
+        return (hh * 4 + y, x * 8 + zz * 2 + kk)
 
     barrier = pltpu.get_barrier_semaphore()
 
@@ -84,13 +90,18 @@
         pl.semaphore_signal(barrier, inc=1, device_id=dev, device_id_type=MESH)
 
     for step in range(1, NH * NZ):
-        greet(ring((place + step) % (NH * NZ)))
+        for core in range(NK):
+            greet(ring((place + step) % (NH * NZ), core))
+    for step in range(1, NY):
+        for turn in range(NX):
+            greet(plane((yy + step) % NY, (xx + turn) % NX))
     for step in range(1, NX):
         greet(xdev((xx + step) % NX))
-    for step in range(1, NY):
-        greet(ydev((yy + step) % NY))
     for step in range(NX):
         greet(xdev((xx + step) % NX, 1 - kk))
+    tiles = NX * NZ * NK
+    greet((layer, (tile + 1) % tiles))
+    greet((layer, (tile + tiles - 1) % tiles))
 
     v_copy = pltpu.make_async_copy(v_hbm, v_buf.at[:, pl.ds(0, klayer)], v_sem)
     v_copy.start()
@@ -120,15 +131,21 @@
     )
     w_buf[...] = (placed * factor).astype(jnp.bfloat16)
 
-    def clear(step, carry):
-        for t_buf in t_bufs:
-            t_buf[step // 8, step // 2 % 4, step % 2, ROWS:, :] = jnp.zeros((PAD - ROWS, t_buf.shape[-1]), jnp.bfloat16)
-        return carry
-
-    lax.fori_loop(0, NX * NZ * NK, clear, 0)
-
     part_a = pl.ds(0, A_ROWS)
-    part_b = pl.ds(A_ROWS, ROWS - A_ROWS)
+
+    def b_rows(u, z0, act):
+        if u == 0:
+            act(pl.ds(A_ROWS, ROWS - A_ROWS))
+            return
+        wide = (z0 == NZ - 1) & (kk == 1)
+
+        @pl.when(wide)
+        def _():
+            act(pl.ds(A_ROWS, ROWS - A_ROWS))
+
+        @pl.when(jnp.logical_not(wide))
+        def _():
+            act(pl.ds(A_ROWS, FEW - A_ROWS))
 
     def copy(src, dst, ssem, rsem, dev):
         return pltpu.make_async_remote_copy(
@@ -144,8 +161,8 @@
     def az(u, z0, way):
         return same(t_bufs[u].at[z0, xx, kk, part_a], kind(u, 0 if way > 0 else 7), az_r.at[u, z0], zdev(zz + way))
 
-    def bz(u, z0, way):
-        return same(t_bufs[u].at[z0, :, kk, part_b], kind(u, 1 if way > 0 else 8), bz_r.at[u, z0], zdev(zz + way))
+    def bz(u, z0, way, rows):
+        return same(t_bufs[u].at[z0, :, kk, rows], kind(u, 1 if way > 0 else 8), bz_r.at[u, z0], zdev(zz + way))
 
     def turn(u, z0):
         return 1 - 2 * ((u + z0) % 2)
@@ -161,16 +178,16 @@
     def ax_far(u, z0):
         return same(t_bufs[u].at[z0, (xx + 2) % 4, kk, part_a], kind(u, 2), ax_r.at[u, z0, 1], sib)
 
-    def bx(u, way):
+    def bx(u, way, rows):
         s = turn(u, 0) if way == 2 else 1 - 2 * way
         source = (xx - s + 4) % 4 if way == 2 else xx
-        return same(t_bufs[u].at[zz, source, kk, part_b], kind(u, 3), bx_r.at[u, way // 2], xdev((xx + s + 4) % 4))
-
-    def bx_near(u):
-        return same(t_bufs[u].at[zz, 0:2, kk, part_b], kind(u, 3), bx_r.at[u, 0], sib)
-
-    def bx_far(u):
-        return same(t_bufs[u].at[zz, (xx + 2) % 4, kk, part_b], kind(u, 3), bx_r.at[u, 1], sib)
+        return same(t_bufs[u].at[zz, source, kk, rows], kind(u, 3), bx_r.at[u, way // 2], xdev((xx + s + 4) % 4))
+
+    def bx_near(u, rows):
+        return same(t_bufs[u].at[zz, 0:2, kk, rows], kind(u, 3), bx_r.at[u, 0], sib)
+
+    def bx_far(u, rows):
+        return same(t_bufs[u].at[zz, (xx + 2) % 4, kk, rows], kind(u, 3), bx_r.at[u, 1], sib)
 
     def sb(u, z0):
         return same(t_bufs[u].at[z0, :, kk, 0:ROWS], kind(u, 4), sib_r.at[u, z0], sib)
@@ -217,11 +234,11 @@
 
     def row_step(u, distance):
         def act(z0, sign):
-            if distance == 0:
-                bx_far(u).wait_recv()
-            else:
-                bz(u, z0, 0).wait_recv()
-            pass_on(sign, lambda way: bz(u, z0, way).start())
+            def hop(rows):
+                (bx_far(u, rows) if distance == 0 else bz(u, z0, 0, rows)).wait_recv()
+                pass_on(sign, lambda way: bz(u, z0, way, rows).start())
+
+            b_rows(u, z0, hop)
             ax_far(u, z0).wait_recv()
             sb(u, z0).start()
 
@@ -231,7 +248,10 @@
         j, cores = UNITS[u]
         n, lanes = len(cores), LANES[u]
         q = lax.broadcasted_iota(jnp.int32, (1, lanes), 1)
-        q_y, q_h, q_z, q_k, q_x = q // (32 * n), q // (16 * n) % 2, q // (4 * n) % 4, q // 4 % n + cores[0], q % 4
+        if u == LAST:
+            q_y, q_x, q_h, q_z, q_k = q // 32, q // 8 % 4, q // 4 % 2, q % 4, cores[0]
+        else:
+            q_y, q_h, q_z, q_k, q_x = q // (32 * n), q // (16 * n) % 2, q // (4 * n) % 4, q // 4 % n + cores[0], q % 4
         pair = (q_h * 4 + q_y) * 128 + (q_x * 8 + q_z * 2 + q_k) * 4 + j
         pick = lax.broadcasted_iota(jnp.int32, (tau_ref.shape[1], lanes), 0) == pair
         block = jnp.dot(
@@ -241,26 +261,23 @@
 
     def own_send(u):
         pass_on(0, lambda way: az(u, zz, way).start())
-        bx(u, 0).start()
-        bx(u, 1).start()
+        b_rows(u, zz, lambda rows: (bx(u, 0, rows).start(), bx(u, 1, rows).start()))
         ax(u, zz, 0).start()
         ax(u, zz, 1).start()
 
     def bx_step(u):
-        bx_near(u).wait_recv()
-        bx(u, 2).start()
-
-    def turn_v(step):
+        b_rows(u, zz, lambda rows: (bx_near(u, rows).wait_recv(), bx(u, 2, rows).start()))
+
+    def turn_v(z0):
         def one(i, carry):
-            t = step * 16 + i
+            t = i // NK * (NZ * NK) + z0 * NK + i % NK
             first = pl.multiple_of((kpiece * t) // 16 * 16, 16)
-            block = (t // 2 % NZ * NX + t // 8) * NK + t % NK
-            lanes = pl.ds(pl.multiple_of(block * PAD, PAD), PAD)
+            lanes = pl.ds(pl.multiple_of((z0 * NX * NK + i) * PAD, PAD), PAD)
             for s in range(v_buf.shape[0]):
                 vt_buf[s * 128 : (s + 1) * 128, lanes] = v_buf[s, pl.ds(first, PAD), :].T
             return carry
 
-        lax.fori_loop(0, 16, one, 0)
+        lax.fori_loop(0, NX * NK, one, 0)
 
     def multiply(u, distance):
         depth = NX * NK * PAD
@@ -290,10 +307,95 @@
             for s in range(v_buf.shape[0]):
                 rows = slice(s * 128, s * 128 + 128)
                 r_buf[lanes, rows] = (accs[u][rows, lanes] * scales_ref[s]).T
+        if u == LAST:
+            for turn, step in ((2, 2), (2, 1), (2, 3), (1, 2), (3, 2), (1, 1), (3, 3), (1, 3), (3, 1)):
+                plane_send(u, step, turn)
+            for step in (2, 1, 3):
+                plane_send(u, step, 0)
+                plane_send(u, 0, step)
+            return
         for step in (2, 1, 3):
             other = (yy + step) % NY
             rows = pl.ds(pl.multiple_of(other * quarter, quarter), quarter)
             copy(r_buf.at[rows], y_bufs[u].at[3 - step], kind(u, 5), y_r.at[u], ydev(other)).start()
+
+    def plane_send(u, step, turn):
+        y, x = (yy + step) % NY, (xx + turn) % NX
+        rows = pl.ds(pl.multiple_of((y * NX + x) * 8, 8), 8)
+        copy(r_bufs[u].at[rows], y_bufs[u].at[yy * NX + xx], kind(u, 5), y_r.at[u], plane(y, x)).start()
+
+    def last_z(u):
+        r_buf, y_buf, q_buf, z_buf = r_bufs[u], y_bufs[u], q_bufs[u], z_bufs[u]
+        core = UNITS[u][1][0]
+        mine = yy * NX + xx
+        y_buf[mine] = r_buf[pl.ds(pl.multiple_of(mine * 8, 8), 8), :]
+        same(y_buf.at[0 : NY * NX - 1], kind(u, 5), y_r.at[u], sib).wait_recv()
+        for x in range(NX):
+            total = y_buf[x] + y_buf[NX + x] + y_buf[2 * NX + x] + y_buf[3 * NX + x]
+            for other in range(NH * NZ):
+                q_buf[other, x : x + 1, :] = total[other : other + 1, :]
+
+        def send(other):
+            copy(q_buf.at[other], z_buf.at[place * NK + kk], kind(u, 6), z_r.at[u], ring(other, core)).start()
+
+        for step in (4, 3, 5, 2, 6, 1, 7):
+            send((place + step) % (NH * NZ))
+
+        @pl.when(kk == core)
+        def _():
+            z_buf[place * NK + kk] = q_buf[place]
+
+        @pl.when(kk != core)
+        def _():
+            send(place)
+
+    def last_own(u):
+        z_buf = z_bufs[u]
+        j, (core,) = UNITS[u]
+
+        @pl.when(kk == core)
+        def _():
+            same(z_buf.at[0 : NH * NZ * NK - 1], kind(u, 6), z_r.at[u], sib).wait_recv()
+            for z in range(NZ):
+                for k in range(NK):
+                    both = z_buf[z * NK + k] + z_buf[(NZ + z) * NK + k]
+                    for x in range(NX):
+                        own_buf[j, x * NK + k, z : z + 1, :] = both[x : x + 1, :]
+
+    def finish(p):
+        width = ab_ref.shape[1]
+        owned = own_buf[p].reshape(NX * NK * NZ, own_buf.shape[3])
+        residual = jnp.zeros(ab_ref.shape, jnp.float32)
+        for s in range(v_buf.shape[0]):
+            residual += jnp.dot(
+                pick_buf[s],
+                owned[:, s * width : (s + 1) * width],
+                precision=lax.Precision.HIGHEST,
+                preferred_element_type=jnp.float32,
+            )
+        out_ref[:, p, :] = residual / (ab_ref[...] - pair_ref[p])
+
+    def x_done(u):
+        j, cores = UNITS[u]
+        for core in range(NK):
+            if core in cores:
+
+                @pl.when(kk == core)
+                def _():
+                    same(own_buf.at[j, 0 : NX * NK - 1], kind(u, 9), x_r.at[u], sib).wait_recv()
+
+        if len(cores) == NK:
+            sent(s_buf.at[j, 0 : NX * NK - 1], kind(u, 9))
+            finish(j)
+            return
+
+        @pl.when(kk == cores[0])
+        def _():
+            sent(s_buf.at[j, 0 : NX - 1], kind(u, 9))
+
+        @pl.when(kk != cores[0])
+        def _():
+            sent(s_buf.at[j, 0:NX], kind(u, 9))
 
     def zs_step(u):
         r_buf, y_buf, q_buf, z_buf = r_bufs[u], y_bufs[u], q_bufs[u], z_bufs[u]
@@ -321,7 +423,7 @@
 
         def send(core, step):
             other = (xx + step) % NX
-            copy(s_buf.at[j, core * NX + other], own_buf.at[j, xx * NK + kk], x_s, x_r, xdev(other, core)).start()
+            copy(s_buf.at[j, core * NX + other], own_buf.at[j, xx * NK + kk], kind(u, 9), x_r.at[u], xdev(other, core)).start()
 
         for core in cores:
 
@@ -342,17 +444,31 @@
     def gather_sent(u):
         t_buf = t_bufs[u]
         sent(t_buf.at[0:3, :, 0, part_a], kind(u, 2))
-        sent(t_buf.at[0:3, 0, 0, part_b], kind(u, 3))
+        b_rows(u, zz, lambda rows: sent(t_buf.at[0:3, 0, 0, rows], kind(u, 3)))
         sent(t_buf.at[:, :, 0, 0:ROWS], kind(u, 4))
 
         for v in range(NZ):
 
             @pl.when(zz == v)
             def _():
-                for count, i in ((v + 1 if v < NZ - 1 else 0, 0), (NZ - v if v > 0 else 0, 7)):
-                    if count:
-                        sent(t_buf.at[0, 0:count, 0, part_a], kind(u, i))
-                        sent(t_buf.at[:, 0:count, 0, part_b], kind(u, i + 1))
+                ups, downs = v + 1 if v < NZ - 1 else 0, NZ - v if v > 0 else 0
+                few = pl.ds(A_ROWS, (ROWS if u == 0 else FEW) - A_ROWS)
+                if ups:
+                    sent(t_buf.at[0, 0:ups, 0, part_a], kind(u, 0))
+                    sent(t_buf.at[:, 0:ups, 0, few], kind(u, 1))
+                if downs:
+                    sent(t_buf.at[0, 0:downs, 0, part_a], kind(u, 7))
+                if downs and u == 0:
+                    sent(t_buf.at[:, 0:downs, 0, few], kind(u, 8))
+                elif downs:
+
+                    @pl.when(kk == 1)
+                    def _():
+                        sent(t_buf.at[0, :, 0, 0 : (FEW - A_ROWS) * downs + ROWS - FEW], kind(u, 8))
+
+                    @pl.when(kk != 1)
+                    def _():
+                        sent(t_buf.at[:, 0:downs, 0, few], kind(u, 8))
 
     def slot_pick():
         slots, owners = v_buf.shape[0], NX * NK * NZ
@@ -374,10 +490,28 @@
             pick_buf[s] = jnp.where(mine[0:1, :] == j, 1.0, 0.0)
 
     own_fill(0)
+    pl.semaphore_wait(barrier, (NX - 1) + (NY - 1) * NX + (NH * NZ - 1) * NK + NX + 2)
+    gives, gets = tile % 16 != 15, tile % 16 != 0
+    edge = copy(w_buf.at[FEW:ROWS], edge_buf, edge_sem.at[0], edge_sem.at[1], (layer, (tile + 1) % tiles))
+
+    @pl.when(gives)
+    def _():
+        edge.start()
+
+    own_send(0)
+
+    @pl.when(gives)
+    def _():
+        edge.wait_send()
+        w_buf[FEW:ROWS, :] = jnp.zeros((ROWS - FEW, w_buf.shape[1]), w_buf.dtype)
+
+    @pl.when(gets)
+    def _():
+        edge.wait_recv()
+        both = w_buf[0 : ROWS - FEW, :].astype(jnp.float32) + edge_buf[...].astype(jnp.float32)
+        w_buf[0 : ROWS - FEW, :] = both.astype(w_buf.dtype)
+
     own_fill(1)
-    slot_pick()
-    pl.semaphore_wait(barrier, (NX - 1) + (NY - 1) + (NH * NZ - 1) + NX)
-    own_send(0)
 
     for tick in range(COUNT + 8):
 
@@ -396,32 +530,43 @@
         at(5, lambda u: row_step(u, 3))
         at(6, lambda u: multiply(u, 3))
         at(6, y_step)
-        at(7, zs_step)
-        at(8, xs_step)
+        at(7, lambda u: last_z(u) if u == LAST else zs_step(u))
+        at(8, lambda u: last_own(u) if u == LAST else xs_step(u))
+        at(9, lambda u: None if u == LAST else x_done(u))
+        if tick == 1:
+            v_copy.wait()
+        if 1 <= tick <= NZ:
+            turn_v((zz + (0, 1, 3, 2)[tick - 1]) % NZ)
+        at(-2, own_fill)
         if tick == 0:
-            v_copy.wait()
-        if tick < 2:
-            turn_v(tick)
-        at(-2, own_fill)
+            def clear(step, carry):
+                for t_buf in t_bufs:
+                    t_buf[step // 8, step // 2 % 4, step % 2, ROWS:, :] = jnp.zeros((PAD - ROWS, t_buf.shape[-1]), jnp.bfloat16)
+
+                @pl.when((step % 2 == kk) & jnp.logical_not((step // 8 == NZ - 1) & (kk == 1)))
+                def _():
+                    for t_buf in t_bufs[1:]:
+                        t_buf[step // 8, step // 2 % 4, step % 2, FEW:ROWS, :] = jnp.zeros((ROWS - FEW, t_buf.shape[-1]), jnp.bfloat16)
+
+                return carry
+
+            lax.fori_loop(0, NX * NZ * NK, clear, 0)
+            slot_pick()
         at(6, gather_sent)
 
-    for u in range(COUNT):
+    finish(UNITS[LAST][0])
+    for u in range(LAST):
         sent(r_bufs[u].at[0 : r_bufs[u].shape[0] // 4 * 3], kind(u, 5))
         sent(q_bufs[u].at[0 : NH * NZ - 1], kind(u, 6))
-    sent(s_buf.at[:, 0 : NX * NK - 1], x_s)
-    same(own_buf.at[:, 0 : NX * NK - 1], x_s, x_r, sib).wait_recv()
-    width = ab_ref.shape[1]
-    for p in range(own_buf.shape[0]):
-        owned = own_buf[p].reshape(NX * NK * NZ, own_buf.shape[3])
-        residual = jnp.zeros(ab_ref.shape, jnp.float32)
-        for s in range(v_buf.shape[0]):
-            residual += jnp.dot(
-                pick_buf[s],
-                owned[:, s * width : (s + 1) * width],
-                precision=lax.Precision.HIGHEST,
-                preferred_element_type=jnp.float32,
-            )
-        out_ref[:, p, :] = residual / (ab_ref[...] - pair_ref[p])
+    sent(r_bufs[LAST].at[0 : (NY * NX - 1) * 8], kind(LAST, 5))
+
+    @pl.when(kk == UNITS[LAST][1][0])
+    def _():
+        sent(q_bufs[LAST].at[0 : NH * NZ - 1], kind(LAST, 6))
+
+    @pl.when(kk != UNITS[LAST][1][0])
+    def _():
+        sent(q_bufs[LAST], kind(LAST, 6))
 
 
 def local(tau, vvvv, scales, tile_ids, counts, spin_c, spin_d, pair_energy, ab_energy):
@@ -448,15 +593,18 @@
             pltpu.VMEM((slots, klayer + 16, width), bf16),
             pltpu.VMEM((columns, ntile * PAD), bf16),
             pltpu.VMEM((ROWS, pairs), bf16),
+            pltpu.VMEM((ROWS - FEW, pairs), bf16),
             [pltpu.VMEM((columns, lanes), f32) for lanes in LANES],
             [pltpu.VMEM((lanes, columns), f32) for lanes in LANES],
-            [pltpu.VMEM((NY - 1, lanes // NY, columns), f32) for lanes in LANES],
+            [pltpu.VMEM((NY - 1, lanes // NY, columns), f32) for lanes in LANES[:LAST]]
+            + [pltpu.VMEM((NY * NX, NH * NZ, columns), f32)],
             [pltpu.VMEM((NH * NZ, lanes // 32, columns), f32) for lanes in LANES],
-            [pltpu.VMEM((NH * NZ, lanes // 32, columns), f32) for lanes in LANES],
+            [pltpu.VMEM((NH * NZ, lanes // 32, columns), f32) for lanes in LANES[:LAST]]
+            + [pltpu.VMEM((NH * NZ * NK, NX, columns), f32)],
             pltpu.VMEM((own_pairs, NX * NK, NZ, columns), f32),
             dma,
-            dma((COUNT, 9)),
-            dma,
+            dma((2,)),
+            dma((COUNT, 10)),
             dma((COUNT, NZ)),
             dma((COUNT, NZ, 2)),
             dma((COUNT, 2)),
@@ -464,7 +612,7 @@
             dma((COUNT, NZ)),
             dma((COUNT,)),
             dma((COUNT,)),
-            dma,
+            dma((COUNT,)),
         ],
         compiler_params=pltpu.CompilerParams(
             collective_id=0, has_side_effects=True, vmem_limit_bytes=56 * 1024 * 1024

time: 103 us -> 100 us (0.971)
  Pallas kernels: 101 us -> 98.7 us
    pallas_call x1, Pallas kernels: 101 us -> 98.7 us  [local(): pl.pallas_call(ladder_kernel, out_shape=jax.ShapeDtypeStruct((all_slots,...]
where the time goes in v4:
time: 100 us
  Pallas kernels  98.7 us (99%)
  local copies, waits for them, and re-layouts  1.67 us (2%)
    pallas_call x1, Pallas kernels, local(): pl.pallas_call(ladder_kernel, out_shape=jax.ShapeDtypeStruct((all_slots,...  98.7 us

profile of v4, /device:TPU:1, one launch (start us, length us, event | category | flops | bytes accessed | tf_op | source)
XLA Modules:
  0.0 100.3 jit_solution(17064446771230660712)
XLA Ops:
  0.0 98.7 %ladder.1 = f32[128,4,128]{2,1,0:T(4,128)} custom-call(bf16[225,1024]{1,0:T(8,128)(2,1)} %bitcast.7, bf16[4,7200,128]{2,1,0:T(8,128)(2,1)} %bitcast.5, f32[4]{0:T(128)} %scales_ref.1, s32[48]{0:T(128)} %spin_c_ref.1, s32[1200]{0:T(1024)} %spin_d_ref.1, s32[128]{0:T(128)} %ids_ref.1, s32[32]{0:T(128)} %counts_ref.1, f32[4]{0:T(128)} %pair_ref.1, ...), custom_call_target="tpu_custom_call" | custom-call | tf_op jit(solution)/shard_map/ladder/pallas_call | solution.py:584
  98.7 1.7 %copy.11 = f32[4,16384]{1,0:T(4,128)} copy(f32[4,16384]{1,0:T(4,128)} %bitcast.6) | data formatting | bytes 524288

commit v5 on v4

--- a/solution.py
+++ b/solution.py
@@ -10,9 +10,10 @@
 MESH = pl.DeviceIdType.MESH
 
 NX, NZ, NK, NY, NH = 4, 4, 2, 4, 2
-UNITS = ((3, (0,)), (0, (0, 1)), (1, (0, 1)), (2, (0, 1)), (3, (1,)))
+UNITS = ((0, (0, 1)), (1, (0, 1)), (2, (0, 1)), (3, (0,)), (3, (1,)))
 LANES = tuple(128 * len(cores) for _, cores in UNITS)
 COUNT = len(UNITS)
+DIRECT = (4,)
 LAST = COUNT - 1
 ROWS = 240
 FEW = 224
@@ -78,11 +79,8 @@
     def ydev(y):
         return (hh * 4 + y, tile)
 
-    def ring(other, core=None):
-        return (other // NZ * 4 + yy, xx * 8 + other % NZ * 2 + (kk if core is None else core))
-
-    def plane(y, x):
-        return (hh * 4 + y, x * 8 + zz * 2 + kk)
+    def ring(other):
+        return (other // NZ * 4 + yy, xx * 8 + other % NZ * 2 + kk)
 
     barrier = pltpu.get_barrier_semaphore()
 
@@ -90,11 +88,9 @@
         pl.semaphore_signal(barrier, inc=1, device_id=dev, device_id_type=MESH)
 
     for step in range(1, NH * NZ):
-        for core in range(NK):
-            greet(ring((place + step) % (NH * NZ), core))
+        greet(ring((place + step) % (NH * NZ)))
     for step in range(1, NY):
-        for turn in range(NX):
-            greet(plane((yy + step) % NY, (xx + turn) % NX))
+        greet(ydev((yy + step) % NY))
     for step in range(1, NX):
         greet(xdev((xx + step) % NX))
     for step in range(NX):
@@ -219,7 +215,8 @@
     def z_step(u, distance):
         def act(z0, sign):
             az(u, z0, 0).wait_recv()
-            pass_on(sign, lambda way: az(u, z0, way).start())
+            if u not in DIRECT:
+                pass_on(sign, lambda way: az(u, z0, way).start())
             ax(u, z0, 0).start()
             ax(u, z0, 1).start()
 
@@ -236,7 +233,11 @@
         def act(z0, sign):
             def hop(rows):
                 (bx_far(u, rows) if distance == 0 else bz(u, z0, 0, rows)).wait_recv()
-                pass_on(sign, lambda way: bz(u, z0, way, rows).start())
+                if u not in DIRECT:
+                    pass_on(sign, lambda way: bz(u, z0, way, rows).start())
+                elif distance == 0:
+                    for d in (3, 2, 1):
+                        sides(d, lambda _, side: bz(u, zz, side * d, rows).start())
 
             b_rows(u, z0, hop)
             ax_far(u, z0).wait_recv()
@@ -248,10 +249,7 @@
         j, cores = UNITS[u]
         n, lanes = len(cores), LANES[u]
         q = lax.broadcasted_iota(jnp.int32, (1, lanes), 1)
-        if u == LAST:
-            q_y, q_x, q_h, q_z, q_k = q // 32, q // 8 % 4, q // 4 % 2, q % 4, cores[0]
-        else:
-            q_y, q_h, q_z, q_k, q_x = q // (32 * n), q // (16 * n) % 2, q // (4 * n) % 4, q // 4 % n + cores[0], q % 4
+        q_y, q_h, q_z, q_k, q_x = q // (32 * n), q // (16 * n) % 2, q // (4 * n) % 4, q // 4 % n + cores[0], q % 4
         pair = (q_h * 4 + q_y) * 128 + (q_x * 8 + q_z * 2 + q_k) * 4 + j
         pick = lax.broadcasted_iota(jnp.int32, (tau_ref.shape[1], lanes), 0) == pair
         block = jnp.dot(
@@ -260,7 +258,11 @@
         t_bufs[u][zz, xx, kk, 0:ROWS, :] = block.astype(jnp.bfloat16)
 
     def own_send(u):
-        pass_on(0, lambda way: az(u, zz, way).start())
+        if u in DIRECT:
+            for d in (3, 2, 1):
+                sides(d, lambda z0, sign: az(u, zz, sign * d).start())
+        else:
+            pass_on(0, lambda way: az(u, zz, way).start())
         b_rows(u, zz, lambda rows: (bx(u, 0, rows).start(), bx(u, 1, rows).start()))
         ax(u, zz, 0).start()
         ax(u, zz, 1).start()
@@ -307,60 +309,10 @@
             for s in range(v_buf.shape[0]):
                 rows = slice(s * 128, s * 128 + 128)
                 r_buf[lanes, rows] = (accs[u][rows, lanes] * scales_ref[s]).T
-        if u == LAST:
-            for turn, step in ((2, 2), (2, 1), (2, 3), (1, 2), (3, 2), (1, 1), (3, 3), (1, 3), (3, 1)):
-                plane_send(u, step, turn)
-            for step in (2, 1, 3):
-                plane_send(u, step, 0)
-                plane_send(u, 0, step)
-            return
         for step in (2, 1, 3):
             other = (yy + step) % NY
             rows = pl.ds(pl.multiple_of(other * quarter, quarter), quarter)
             copy(r_buf.at[rows], y_bufs[u].at[3 - step], kind(u, 5), y_r.at[u], ydev(other)).start()
-
-    def plane_send(u, step, turn):
-        y, x = (yy + step) % NY, (xx + turn) % NX
-        rows = pl.ds(pl.multiple_of((y * NX + x) * 8, 8), 8)
-        copy(r_bufs[u].at[rows], y_bufs[u].at[yy * NX + xx], kind(u, 5), y_r.at[u], plane(y, x)).start()
-
-    def last_z(u):
-        r_buf, y_buf, q_buf, z_buf = r_bufs[u], y_bufs[u], q_bufs[u], z_bufs[u]
-        core = UNITS[u][1][0]
-        mine = yy * NX + xx
-        y_buf[mine] = r_buf[pl.ds(pl.multiple_of(mine * 8, 8), 8), :]
-        same(y_buf.at[0 : NY * NX - 1], kind(u, 5), y_r.at[u], sib).wait_recv()
-        for x in range(NX):
-            total = y_buf[x] + y_buf[NX + x] + y_buf[2 * NX + x] + y_buf[3 * NX + x]
-            for other in range(NH * NZ):
-                q_buf[other, x : x + 1, :] = total[other : other + 1, :]
-
-        def send(other):
-            copy(q_buf.at[other], z_buf.at[place * NK + kk], kind(u, 6), z_r.at[u], ring(other, core)).start()
-
-        for step in (4, 3, 5, 2, 6, 1, 7):
-            send((place + step) % (NH * NZ))
-
-        @pl.when(kk == core)
-        def _():
-            z_buf[place * NK + kk] = q_buf[place]
-
-        @pl.when(kk != core)
-        def _():
-            send(place)
-
-    def last_own(u):
-        z_buf = z_bufs[u]
-        j, (core,) = UNITS[u]
-
-        @pl.when(kk == core)
-        def _():
-            same(z_buf.at[0 : NH * NZ * NK - 1], kind(u, 6), z_r.at[u], sib).wait_recv()
-            for z in range(NZ):
-                for k in range(NK):
-                    both = z_buf[z * NK + k] + z_buf[(NZ + z) * NK + k]
-                    for x in range(NX):
-                        own_buf[j, x * NK + k, z : z + 1, :] = both[x : x + 1, :]
 
     def finish(p):
         width = ab_ref.shape[1]
@@ -396,6 +348,9 @@
         @pl.when(kk != cores[0])
         def _():
             sent(s_buf.at[j, 0:NX], kind(u, 9))
+
+        if u != LAST and all(place != j for place, _ in UNITS[u + 1 :]):
+            finish(j)
 
     def zs_step(u):
         r_buf, y_buf, q_buf, z_buf = r_bufs[u], y_bufs[u], q_bufs[u], z_bufs[u]
@@ -451,6 +406,12 @@
 
             @pl.when(zz == v)
             def _():
+                if u in DIRECT:
+                    for count, i in ((NZ - 1 - v, 0), (v, 7)):
+                        if count:
+                            sent(t_buf.at[0, 0:count, 0, part_a], kind(u, i))
+                            b_rows(u, v, lambda rows: sent(t_buf.at[:, 0:count, 0, rows], kind(u, i + 1)))
+                    return
                 ups, downs = v + 1 if v < NZ - 1 else 0, NZ - v if v > 0 else 0
                 few = pl.ds(A_ROWS, (ROWS if u == 0 else FEW) - A_ROWS)
                 if ups:
@@ -490,7 +451,7 @@
             pick_buf[s] = jnp.where(mine[0:1, :] == j, 1.0, 0.0)
 
     own_fill(0)
-    pl.semaphore_wait(barrier, (NX - 1) + (NY - 1) * NX + (NH * NZ - 1) * NK + NX + 2)
+    pl.semaphore_wait(barrier, (NX - 1) + (NY - 1) + (NH * NZ - 1) + NX + 2)
     gives, gets = tile % 16 != 15, tile % 16 != 0
     edge = copy(w_buf.at[FEW:ROWS], edge_buf, edge_sem.at[0], edge_sem.at[1], (layer, (tile + 1) % tiles))
 
@@ -513,26 +474,33 @@
 
     own_fill(1)
 
-    for tick in range(COUNT + 8):
-
-        def at(stage, act):
-            if 0 <= tick - stage < COUNT:
-                act(tick - stage)
+    for tick in range(COUNT + 9):
+
+        def at(stage, act, direct=None):
+            u = tick - stage
+            if 0 <= u < COUNT and direct in (None, u in DIRECT):
+                act(u)
 
         at(-1, own_send)
-        at(1, lambda u: (bx_step(u), z_step(u, 1), far_step(u, 0)))
+        at(1, lambda u: (bx_step(u), z_step(u, 1), far_step(u, 0)), False)
+        at(1, lambda u: (bx_step(u), far_step(u, 0), z_step(u, 1), z_step(u, 2), z_step(u, 3)), True)
         at(3, lambda u: multiply(u, 0))
-        at(2, lambda u: (row_step(u, 0), far_step(u, 1), z_step(u, 2)))
+        at(2, lambda u: (row_step(u, 0), far_step(u, 1), z_step(u, 2)), False)
+        at(2, lambda u: (row_step(u, 0), far_step(u, 1), far_step(u, 2), far_step(u, 3)), True)
         at(4, lambda u: multiply(u, 1))
-        at(3, lambda u: (row_step(u, 1), far_step(u, 2), z_step(u, 3)))
-        at(5, lambda u: multiply(u, 2))
-        at(4, lambda u: (row_step(u, 2), far_step(u, 3)))
-        at(5, lambda u: row_step(u, 3))
-        at(6, lambda u: multiply(u, 3))
-        at(6, y_step)
-        at(7, lambda u: last_z(u) if u == LAST else zs_step(u))
-        at(8, lambda u: last_own(u) if u == LAST else xs_step(u))
-        at(9, lambda u: None if u == LAST else x_done(u))
+        at(3, lambda u: (row_step(u, 1), far_step(u, 2), z_step(u, 3)), False)
+        at(3, lambda u: (row_step(u, 1), row_step(u, 2), row_step(u, 3)), True)
+        at(5, lambda u: multiply(u, 2), False)
+        at(4, lambda u: (row_step(u, 2), far_step(u, 3)), False)
+        at(5, lambda u: row_step(u, 3), False)
+        at(6, lambda u: (multiply(u, 3), y_step(u)), False)
+        at(4, lambda u: (multiply(u, 2), multiply(u, 3), y_step(u)), True)
+        at(7, zs_step, False)
+        at(5, zs_step, True)
+        at(8, xs_step, False)
+        at(6, xs_step, True)
+        at(9, x_done, False)
+        at(7, x_done, True)
         if tick == 1:
             v_copy.wait()
         if 1 <= tick <= NZ:
@@ -552,21 +520,13 @@
 
             lax.fori_loop(0, NX * NZ * NK, clear, 0)
             slot_pick()
-        at(6, gather_sent)
+        at(6, gather_sent, False)
+        at(4, gather_sent, True)
 
     finish(UNITS[LAST][0])
-    for u in range(LAST):
+    for u in range(COUNT):
         sent(r_bufs[u].at[0 : r_bufs[u].shape[0] // 4 * 3], kind(u, 5))
         sent(q_bufs[u].at[0 : NH * NZ - 1], kind(u, 6))
-    sent(r_bufs[LAST].at[0 : (NY * NX - 1) * 8], kind(LAST, 5))
-
-    @pl.when(kk == UNITS[LAST][1][0])
-    def _():
-        sent(q_bufs[LAST].at[0 : NH * NZ - 1], kind(LAST, 6))
-
-    @pl.when(kk != UNITS[LAST][1][0])
-    def _():
-        sent(q_bufs[LAST], kind(LAST, 6))
 
 
 def local(tau, vvvv, scales, tile_ids, counts, spin_c, spin_d, pair_energy, ab_energy):
@@ -596,11 +556,9 @@
             pltpu.VMEM((ROWS - FEW, pairs), bf16),
             [pltpu.VMEM((columns, lanes), f32) for lanes in LANES],
             [pltpu.VMEM((lanes, columns), f32) for lanes in LANES],
-            [pltpu.VMEM((NY - 1, lanes // NY, columns), f32) for lanes in LANES[:LAST]]
-            + [pltpu.VMEM((NY * NX, NH * NZ, columns), f32)],
+            [pltpu.VMEM((NY - 1, lanes // NY, columns), f32) for lanes in LANES],
             [pltpu.VMEM((NH * NZ, lanes // 32, columns), f32) for lanes in LANES],
-            [pltpu.VMEM((NH * NZ, lanes // 32, columns), f32) for lanes in LANES[:LAST]]
-            + [pltpu.VMEM((NH * NZ * NK, NX, columns), f32)],
+            [pltpu.VMEM((NH * NZ, lanes // 32, columns), f32) for lanes in LANES],
             pltpu.VMEM((own_pairs, NX * NK, NZ, columns), f32),
             dma,
             dma((2,)),

time: 100 us -> 98 us (0.980)
  Pallas kernels: 98.7 us -> 96 us
    pallas_call x1, Pallas kernels: 98.7 us -> 96 us  [local(): pl.pallas_call(ladder_kernel, out_shape=jax.ShapeDtypeStruct((all_slots,...]
where the time goes in v5:
time: 98 us; the launch traced here: 97.7 us
  Pallas kernels  96 us (98%)
  local copies, waits for them, and re-layouts  1.67 us (2%)
    pallas_call x1, Pallas kernels, local(): pl.pallas_call(ladder_kernel, out_shape=jax.ShapeDtypeStruct((all_slots,...  96 us

profile of v5, /device:TPU:1, one launch (start us, length us, event | category | flops | bytes accessed | tf_op | source)
XLA Modules:
  0.0 97.7 jit_solution(9941722823449766030)
XLA Ops:
  0.0 96.0 %ladder.1 = f32[128,4,128]{2,1,0:T(4,128)} custom-call(bf16[225,1024]{1,0:T(8,128)(2,1)} %bitcast.7, bf16[4,7200,128]{2,1,0:T(8,128)(2,1)} %bitcast.5, f32[4]{0:T(128)} %scales_ref.1, s32[48]{0:T(128)} %spin_c_ref.1, s32[1200]{0:T(1024)} %spin_d_ref.1, s32[128]{0:T(128)} %ids_ref.1, s32[32]{0:T(128)} %counts_ref.1, f32[4]{0:T(128)} %pair_ref.1, ...), custom_call_target="tpu_custom_call" | custom-call | tf_op jit(solution)/shard_map/ladder/pallas_call | solution.py:544
  96.0 1.7 %copy.11 = f32[4,16384]{1,0:T(4,128)} copy(f32[4,16384]{1,0:T(4,128)} %bitcast.6) | data formatting | bytes 524288

commit v6 on v5

--- a/solution.py
+++ b/solution.py
@@ -501,6 +501,10 @@
         at(6, xs_step, True)
         at(9, x_done, False)
         at(7, x_done, True)
+        if tick == COUNT + 6:
+            for u in range(COUNT):
+                sent(r_bufs[u].at[0 : r_bufs[u].shape[0] // 4 * 3], kind(u, 5))
+                sent(q_bufs[u].at[0 : NH * NZ - 1], kind(u, 6))
         if tick == 1:
             v_copy.wait()
         if 1 <= tick <= NZ:
@@ -524,9 +528,6 @@
         at(4, gather_sent, True)
 
     finish(UNITS[LAST][0])
-    for u in range(COUNT):
-        sent(r_bufs[u].at[0 : r_bufs[u].shape[0] // 4 * 3], kind(u, 5))
-        sent(q_bufs[u].at[0 : NH * NZ - 1], kind(u, 6))
 
 
 def local(tau, vvvv, scales, tile_ids, counts, spin_c, spin_d, pair_energy, ab_energy):

time: 98 us -> 97.9 us (level)
  no operation moved by 1% of the time
where the time goes in v6:
time: 97.9 us; the launch traced here: 97.7 us
  Pallas kernels  96 us (98%)
  local copies, waits for them, and re-layouts  1.67 us (2%)
    pallas_call x1, Pallas kernels, local(): pl.pallas_call(ladder_kernel, out_shape=jax.ShapeDtypeStruct((all_slots,...  96 us

profile of v6, /device:TPU:1, one launch (start us, length us, event | category | flops | bytes accessed | tf_op | source)
XLA Modules:
  0.0 97.7 jit_solution(16941196874361520631)
XLA Ops:
  0.0 96.0 %ladder.1 = f32[128,4,128]{2,1,0:T(4,128)} custom-call(bf16[225,1024]{1,0:T(8,128)(2,1)} %bitcast.7, bf16[4,7200,128]{2,1,0:T(8,128)(2,1)} %bitcast.5, f32[4]{0:T(128)} %scales_ref.1, s32[48]{0:T(128)} %spin_c_ref.1, s32[1200]{0:T(1024)} %spin_d_ref.1, s32[128]{0:T(128)} %ids_ref.1, s32[32]{0:T(128)} %counts_ref.1, f32[4]{0:T(128)} %pair_ref.1, ...), custom_call_target="tpu_custom_call" | custom-call | tf_op jit(solution)/shard_map/ladder/pallas_call | solution.py:545
  96.0 1.7 %copy.11 = f32[4,16384]{1,0:T(4,128)} copy(f32[4,16384]{1,0:T(4,128)} %bitcast.6) | data formatting | bytes 524288
